TPU v7x, 32 devices: a whole 2x2x4 slice. The times are simulated.
32 devices in a mesh: gx: 2 (over y), gy: 4 (over x, core), gz: 4 (over z).
Axes of the slice: x: 2, y: 2, z: 4, core: 2. Of those that a mesh axis runs over, the one named last changes fastest.
Arguments:
- fields: float32 [6, 32, 64, 512], P(None, 'gx', 'gy', 'gz'), may hold values from -6 to 6
- polarization: float32 [6, 32, 64, 512], P(None, 'gx', 'gy', 'gz'), may hold values from -3 to 3
- material: int32 [32, 64, 512], P('gx', 'gy', 'gz'), may hold values from 0 to 4
- omega0: float32 [4], replicated, may hold values from 0.1 to 0.5
- damping: float32 [4], replicated, may hold values from 0.05 to 0.8
- strength: float32 [4], replicated, may hold values from 0.5 to 2.5
- tile_count: int32 [8, 4], P(('gx', 'gy')), may hold values from 1 to 18, 24 in all within a row
- tile_place: int32 [8, 4, 18], P(('gx', 'gy')), may hold values from 0 to 31, as said below
- dir_angles: float32 [2, 8192], replicated, may hold values from 0 to 3.14159
- dir_order: int32 [8192], replicated, may hold values from 0 to 8191, each once
Outputs:
- fields_out: float32 [6, 32, 64, 512], P(None, 'gx', 'gy', 'gz')
- far_field: float32 [8192, 8], P(('gx', 'gy', 'gz'))
Inputs may be any that keep to these rules, and one draw needn't show every extreme that they name: `tile_count`: for each column g, the 4 counts sum to 24, and the largest of them is exactly 18. `tile_place`: the 18 positions of one device are distinct; only the first tile_count of them are live tiles.
All inputs are finite; a program needn't handle non-finite values.
Results may differ from a plain program's by a relative error of at most 0.0032.
Values may be sent and summed in bfloat16 or wider, within the bound.
A program may use at most 64 MiB of HBM per device.

v0:
```python
import math

import jax
import jax.numpy as jnp
from jax import lax
from jax.sharding import PartitionSpec as P

TY = 8
STEPS = 4
DIRS = 8192
TILE_MEAN = 6


SPEED = 0.5
WAVE = 0.35


def with_halo(block, sides, width):
    for axis, dim in sides:
        count = lax.axis_size(axis)
        forward = [(i, i + 1) for i in range(count - 1)]
        backward = [(target, source) for source, target in forward]
        low = lax.ppermute(
            lax.slice_in_dim(block, block.shape[dim] - width, None, axis=dim), axis, forward
        )
        high = lax.ppermute(lax.slice_in_dim(block, 0, width, axis=dim), axis, backward)
        block = jnp.concatenate([low, block, high], axis=dim)
    return block


def lorentz(omega0, damping, strength):
    denominator = 1.0 + 0.5 * damping
    square = omega0 * omega0
    return (
        (2.0 - square) / denominator,
        -(1.0 - 0.5 * damping) / denominator,
        strength * square / denominator,
    )


def lookup(material, coef_table):
    result = jnp.zeros(material.shape, jnp.float32)
    for mat_index in range(coef_table.shape[0]):
        result = result + jnp.where(material == mat_index + 1, coef_table[mat_index], 0.0)
    return result


def ahead(values, axis_id):
    extent = values.shape[axis_id]
    padded = jnp.pad(
        values, [(0, 1) if other == axis_id else (0, 0) for other in range(values.ndim)]
    )
    return lax.slice_in_dim(padded, 1, extent + 1, axis=axis_id)


def behind(values, axis_id):
    extent = values.shape[axis_id]
    padded = jnp.pad(
        values, [(1, 0) if other == axis_id else (0, 0) for other in range(values.ndim)]
    )
    return lax.slice_in_dim(padded, 0, extent, axis=axis_id)


def magnetic_update(electric, magnetic):
    electric_x, electric_y, electric_z = (electric[0], electric[1], electric[2])
    magnetic_x = magnetic[0] - SPEED * (
        ahead(electric_z, 1) - electric_z - (ahead(electric_y, 2) - electric_y)
    )
    magnetic_y = magnetic[1] - SPEED * (
        ahead(electric_x, 2) - electric_x - (ahead(electric_z, 0) - electric_z)
    )
    magnetic_z = magnetic[2] - SPEED * (
        ahead(electric_y, 0) - electric_y - (ahead(electric_x, 1) - electric_x)
    )
    return jnp.stack([magnetic_x, magnetic_y, magnetic_z])


def curl_back(magnetic):
    magnetic_x, magnetic_y, magnetic_z = (magnetic[0], magnetic[1], magnetic[2])
    curl_x = magnetic_z - behind(magnetic_z, 1) - (magnetic_y - behind(magnetic_y, 2))
    curl_y = magnetic_x - behind(magnetic_x, 2) - (magnetic_z - behind(magnetic_z, 0))
    curl_z = magnetic_y - behind(magnetic_y, 0) - (magnetic_x - behind(magnetic_x, 1))
    return jnp.stack([curl_x, curl_y, curl_z])


def inside_band(offset, extent, total, ghost_depth):
    global_ids = jnp.arange(extent + 2 * ghost_depth) + offset - ghost_depth
    return jnp.where((global_ids >= 0) & (global_ids < total), 1.0, 0.0).astype(jnp.float32)


def tile_patches(values, places, blocks_y):
    width_x, width_y, depth_z = (values.shape[1], values.shape[2], values.shape[3])
    grouped = values.reshape(2, width_x * blocks_y, TY, depth_z)
    return jnp.take(grouped, places, axis=1)


def accumulate(sums, mag_inner, ele_inner, instant, places, blocks_y):
    ele_real, ele_imag, mag_real, mag_imag = sums
    angle_h = WAVE * SPEED * (instant + 0.5)
    angle_e = WAVE * SPEED * (instant + 1.0)
    mag_tiles = tile_patches(mag_inner, places, blocks_y)
    ele_tiles = tile_patches(ele_inner, places, blocks_y)
    mag_real = mag_real + math.cos(angle_h) * mag_tiles
    mag_imag = mag_imag - math.sin(angle_h) * mag_tiles
    ele_real = ele_real + math.cos(angle_e) * ele_tiles
    ele_imag = ele_imag - math.sin(angle_e) * ele_tiles
    return (ele_real, ele_imag, mag_real, mag_imag)


def far_block(currents, tile_x, tile_y, tile_z, directions, rows_y, depth_z):
    row_pos = jnp.arange(rows_y, dtype=jnp.float32)
    depth_pos = jnp.arange(depth_z, dtype=jnp.float32)
    phases = WAVE * (
        directions[1][None, None, :] * row_pos[:, None, None]
        + directions[2][None, None, :] * depth_pos[None, :, None]
    )
    phase_table = jnp.concatenate([jnp.cos(phases), jnp.sin(phases)], axis=2).astype(jnp.bfloat16)
    block_width = directions.shape[1]
    phase_table = phase_table.reshape(rows_y * depth_z, 2 * block_width)
    tiles = currents.shape[0]
    products = jnp.dot(
        currents.reshape(tiles * 8, rows_y * depth_z),
        phase_table,
        preferred_element_type=jnp.float32,
    )
    products = products.reshape(tiles, 4, 2, 2, block_width)
    real_part = products[:, :, 0, 0] - products[:, :, 1, 1]
    imag_part = products[:, :, 0, 1] + products[:, :, 1, 0]
    tile_phase = WAVE * (
        directions[0][None, :] * tile_x[:, None]
        + directions[1][None, :] * tile_y[:, None]
        + directions[2][None, :] * tile_z[:, None]
    )
    tile_cos = jnp.cos(tile_phase)[:, None, :]
    tile_sin = jnp.sin(tile_phase)[:, None, :]
    far_real = jnp.sum(real_part * tile_cos - imag_part * tile_sin, axis=0)
    far_imag = jnp.sum(real_part * tile_sin + imag_part * tile_cos, axis=0)
    return jnp.stack([far_real, far_imag], axis=1).reshape(8, block_width)


def shards(
    fields,
    polarization,
    material,
    omega0,
    damping,
    strength,
    tile_count,
    tile_place,
    dir_angles,
    dir_order,
):
    width_x, width_y, depth_z = (fields.shape[1], fields.shape[2], fields.shape[3])
    blocks_y = width_y // TY
    slot_count = tile_place.shape[2]
    layer_z = lax.axis_index("gz")
    first_x = lax.axis_index("gx") * width_x
    first_y = lax.axis_index("gy") * width_y
    first_z = layer_z * depth_z
    table_a, table_b, table_c = lorentz(omega0, damping, strength)
    coef_a = lookup(material, table_a)
    coef_b = lookup(material, table_b)
    coef_c = lookup(material, table_c)
    sheet_mask = jnp.where(material > 0, 1.0, 0.0).astype(jnp.float32)
    counts = tile_count[0]
    own_places = lax.dynamic_index_in_dim(tile_place[0], layer_z, 0, keepdims=False)
    empty_sum = jnp.zeros((2, slot_count, TY, depth_z), jnp.float32)
    sums = (empty_sum, empty_sum, empty_sum, empty_sum)
    ghost_depth = STEPS
    stacked = jnp.concatenate(
        [fields, polarization, jnp.stack([coef_a, coef_b, coef_c, sheet_mask])], axis=0
    )
    widened = with_halo(stacked, (("gx", 1), ("gy", 2), ("gz", 3)), STEPS)
    inside = (
        inside_band(first_x, width_x, lax.axis_size("gx") * width_x, ghost_depth)[:, None, None]
        * inside_band(first_y, width_y, lax.axis_size("gy") * width_y, ghost_depth)[None, :, None]
        * inside_band(first_z, depth_z, lax.axis_size("gz") * depth_z, ghost_depth)[None, None, :]
    )
    electric = widened[0:3]
    magnetic = widened[3:6]
    pol_now = widened[6:9]
    pol_old = widened[9:12]
    wide_a, wide_b, wide_c, wide_sheet = (widened[12], widened[13], widened[14], widened[15])
    for instant in range(STEPS):
        magnetic = magnetic_update(electric, magnetic) * inside[None]
        saturation = 1.0 / (
            1.0 + electric[0] * electric[0] + electric[1] * electric[1] + electric[2] * electric[2]
        )
        pol_new = wide_a * pol_now + wide_b * pol_old + wide_c * saturation * electric
        electric = (
            electric + SPEED * curl_back(magnetic) - wide_sheet * (pol_new - pol_now)
        ) * inside[None]
        pol_old = pol_now
        pol_now = pol_new
        ele_inner = electric[
            :,
            ghost_depth : ghost_depth + width_x,
            ghost_depth : ghost_depth + width_y,
            ghost_depth : ghost_depth + depth_z,
        ]
        mag_inner = magnetic[
            :,
            ghost_depth : ghost_depth + width_x,
            ghost_depth : ghost_depth + width_y,
            ghost_depth : ghost_depth + depth_z,
        ]
        sums = accumulate(sums, mag_inner[1:3], ele_inner[1:3], instant, own_places, blocks_y)
    field_state = jnp.concatenate([ele_inner, mag_inner], axis=0)
    ele_real, ele_imag, mag_real, mag_imag = sums
    currents = jnp.stack(
        [
            -mag_real[1],
            -mag_imag[1],
            mag_real[0],
            mag_imag[0],
            ele_real[1],
            ele_imag[1],
            -ele_real[0],
            -ele_imag[0],
        ],
        axis=1,
    )
    live_mask = (jnp.arange(slot_count) < counts[layer_z]).astype(jnp.float32)
    currents = (
        (currents * live_mask[:, None, None, None])
        .reshape(slot_count, 8, TY * depth_z)
        .astype(jnp.bfloat16)
    )
    chosen = currents
    tile_z = jnp.zeros((slot_count,), jnp.float32) + first_z.astype(jnp.float32)
    tile_x = (first_x + own_places // blocks_y).astype(jnp.float32)
    tile_y = (first_y + own_places % blocks_y * TY).astype(jnp.float32)
    polar_angle = jnp.take(dir_angles[0], dir_order)
    azimuth = jnp.take(dir_angles[1], dir_order)
    dir_vec = jnp.stack(
        [
            jnp.sin(polar_angle) * jnp.cos(azimuth),
            jnp.sin(polar_angle) * jnp.sin(azimuth),
            jnp.cos(polar_angle),
        ]
    )
    tile_total = lax.axis_size("gx") * lax.axis_size("gy") * lax.axis_size("gz") * TILE_MEAN
    norm_scale = 1.0 / math.sqrt(tile_total * TY * depth_z)
    devices_all = lax.axis_size(("gx", "gy", "gz"))
    block_width = math.gcd(DIRS // devices_all * lax.axis_size(("gx", "gy", "gz")), 512)

    def block_far(offset):
        directions = lax.dynamic_slice_in_dim(dir_vec, offset, block_width, 1)
        return far_block(chosen, tile_x, tile_y, tile_z, directions, TY, depth_z)

    far_blocks = lax.map(
        block_far,
        jnp.arange(
            DIRS // devices_all * lax.axis_size(("gx", "gy", "gz")) // block_width, dtype=jnp.int32
        )
        * block_width,
    )
    far_field = lax.psum_scatter(
        far_blocks.transpose(0, 2, 1).reshape(
            DIRS // devices_all * lax.axis_size(("gx", "gy", "gz")), 8
        )
        * norm_scale,
        ("gx", "gy", "gz"),
        scatter_dimension=0,
        tiled=True,
    )
    return (field_state, far_field)


def solution(mesh):
    placed = (
        P(None, "gx", "gy", "gz"),
        P(None, "gx", "gy", "gz"),
        P("gx", "gy", "gz"),
        P(),
        P(),
        P(),
        P(("gx", "gy"), None),
        P(("gx", "gy"), None, None),
        P(),
        P(),
    )
    return jax.shard_map(
        shards,
        mesh=mesh,
        in_specs=placed,
        out_specs=(P(None, "gx", "gy", "gz"), P(("gx", "gy", "gz"), None)),
        check_vma=False,
    )
```

profile of v0, /device:TPU:0, one launch (start us, length us, event | category | flops | bytes accessed | tf_op | source)
XLA Modules:
  0.0 581.0 jit_solution(5083883528028672944)
XLA Ops:
  7.2 1.3 constant_dynamic-update-slice_fusion.2
  10.7 2.8 bitcast_dynamic-update-slice_fusion.3
  13.5 2.6 bitcast_dynamic-update-slice_fusion.2
  16.1 2.5 bitcast_dynamic-update-slice_fusion.1
  18.6 1.1 fusion.157
  19.6 1.3 collective-permute-start.1
  20.9 5.7 collective-permute-start
  26.8 45.5 %gather_fusion.1 = f32[8192]{0:T(1024)S(1)} fusion(f32[8192]{0:T(1024)S(1)} %bitcast.326, s32[8192]{0:T(1024)S(1)} %fusion.150), kind=kCustom, calls=%fused_computation.2.clone | custom fusion | bytes 98304 | tf_op jit(solution)/shard_map/jit(_take)/gather | solution.py:234
  72.3 45.5 %gather_fusion = f32[8192]{0:T(1024)S(1)} fusion(f32[8192]{0:T(1024)S(1)} %bitcast.325, s32[8192]{0:T(1024)S(1)} %fusion.150), kind=kCustom, calls=%fused_computation.clone | custom fusion | bytes 98304 | tf_op jit(solution)/shard_map/jit(_take)/gather | solution.py:233
  119.0 1.0 broadcast_multiply_fusion.1
  120.0 1.6 pad_maximum_fusion.6
  121.7 1.3 collective-permute-start.3
  123.0 3.9 collective-permute-start.2
  128.0 2.1 pad_maximum_fusion.2
  130.1 5.3 fusion.156
  135.5 4.9 copy.52
  140.3 1.3 collective-permute-start.5
  141.6 4.9 copy.51
  146.5 6.1 %collective-permute-start.4 = (f32[16,24,24,4]{2,1,3,0:T(8,128)}, f32[16,24,24,4]{2,1,3,0:T(8,128)}, u32[]{:S(2)}, u32[]{:S(2)}) collective-permute-start(f32[16,24,24,4]{2,1,3,0:T(8,128)} %copy.51), channel_id=1, source_target_pairs={{0,1},{1,2},{2,3},{4,5},{5,6},{6,7},{8,9},{9,10},{10,11},{12,13},{... | collective-permute-start | bytes 442376 | tf_op jit(solution)/shard_map/ppermute | solution.py:23
  153.3 2.8 collective-permute-done.5
  156.1 4.8 copy.54
  160.9 1.8 collective-permute-done.4
  162.7 4.9 copy.53
  167.7 3.3 multiply_bitcast_fusion.3
  171.0 1.1 copy-done.2
  172.2 1.2 fusion.41
  173.4 1.4 fusion.36
  174.8 1.4 fusion.100
  177.0 9.3 %pad_maximum_fusion.1 = f32[16,24,24,136]{3,2,1,0:T(8,128)S(1)} fusion(f32[16,24,24,4]{3,2,1,0:T(8,128)S(1)} %bitcast.328, f32[16,24,4,128]{3,2,1,0:T(4,128)S(1)} %collective-permute-done.3, f32[16,4,16,128]{3,2,1,0:T(8,128)S(1)} %copy-done.4, f32[16,16,16,128]{3,2,1,0:T(8,128)S(1)} %bitcast_dynamic-update-slice_fusion, ...), kind=kLoop, calls=%fused_computation.39 | loop fusion | flops 7520256 | bytes 10027008 | tf_op jit(solution)/shard_map/concatenate | solution.py:27
  186.3 1.6 maximum_bitcast_fusion.1
  187.9 1.2 maximum_bitcast_fusion
  189.1 5.3 fusion.22
  198.3 1.4 fusion.28
  204.4 2.1 fusion.31
  206.5 1.2 copy-done.6
  208.6 2.2 gather_fusion.9
  210.8 1.2 gather_fusion.8
  212.0 1.2 gather_fusion.7
  213.8 1.5 gather_fusion.5
  215.4 1.2 gather_fusion.4
  217.8 1.3 fusion.137
  219.1 0.9 stack.188
  220.2 208.9 %while.11 = (s32[]{:T(128)}, f32[16,8,512]{2,1,0:T(8,128)S(1)}, s32[16]{0:T(128)S(1)}, f32[3,8192]{1,0:T(4,128)}, bf16[18,8,1024]{2,1,0:T(8,128)(2,1)S(1)}, /*in...) while((s32[]{:T(128)}, f32[16,8,512]{2,1,0:T(8,128)S(1)}, ...), condition=%wide.region_3.6_spmd.clone, body=%wide.region_0.5_spmd.clone.sunk | while | flops 308766208 | bytes 8612207 | solution.py:251
  222.7 0.9 constant_dynamic-slice_fusion.4
  223.7 7.7 %cosine_convert_fusion.2 = (bf16[8,128,512]{2,1,0:T(8,128)(2,1)S(1)}, bf16[8,128,512]{2,1,0:T(8,128)(2,1)S(1)}) fusion(f32[128,512]{1,0:T(8,128)S(1)} %iota_multiply_fusion.5, f32[8,512]{1,0:T(8,128)S(1)} %iota_multiply_fusion.6), kind=kLoop, calls=%fused_computation.16.clone.1 | loop fusion | flops 2097152 | bytes 2375680 | tf_op jit(solution)/shard_map/convert.3
  235.8 0.9 constant_dynamic-slice_fusion.4
  236.8 7.7 %cosine_convert_fusion.2 = (bf16[8,128,512]{2,1,0:T(8,128)(2,1)S(1)}, bf16[8,128,512]{2,1,0:T(8,128)(2,1)S(1)}) fusion(f32[128,512]{1,0:T(8,128)S(1)} %iota_multiply_fusion.5, f32[8,512]{1,0:T(8,128)S(1)} %iota_multiply_fusion.6), kind=kLoop, calls=%fused_computation.16.clone.1 | loop fusion | flops 2097152 | bytes 2375680 | tf_op jit(solution)/shard_map/convert.3
  249.8 7.7 %cosine_convert_fusion.2 = (bf16[8,128,512]{2,1,0:T(8,128)(2,1)S(1)}, bf16[8,128,512]{2,1,0:T(8,128)(2,1)S(1)}) fusion(f32[128,512]{1,0:T(8,128)S(1)} %iota_multiply_fusion.5, f32[8,512]{1,0:T(8,128)S(1)} %iota_multiply_fusion.6), kind=kLoop, calls=%fused_computation.16.clone.1 | loop fusion | flops 2097152 | bytes 2375680 | tf_op jit(solution)/shard_map/convert.3
  262.9 7.7 %cosine_convert_fusion.2 = (bf16[8,128,512]{2,1,0:T(8,128)(2,1)S(1)}, bf16[8,128,512]{2,1,0:T(8,128)(2,1)S(1)}) fusion(f32[128,512]{1,0:T(8,128)S(1)} %iota_multiply_fusion.5, f32[8,512]{1,0:T(8,128)S(1)} %iota_multiply_fusion.6), kind=kLoop, calls=%fused_computation.16.clone.1 | loop fusion | flops 2097152 | bytes 2375680 | tf_op jit(solution)/shard_map/convert.3
  275.9 7.7 %cosine_convert_fusion.2 = (bf16[8,128,512]{2,1,0:T(8,128)(2,1)S(1)}, bf16[8,128,512]{2,1,0:T(8,128)(2,1)S(1)}) fusion(f32[128,512]{1,0:T(8,128)S(1)} %iota_multiply_fusion.5, f32[8,512]{1,0:T(8,128)S(1)} %iota_multiply_fusion.6), kind=kLoop, calls=%fused_computation.16.clone.1 | loop fusion | flops 2097152 | bytes 2375680 | tf_op jit(solution)/shard_map/convert.3
  289.0 7.7 %cosine_convert_fusion.2 = (bf16[8,128,512]{2,1,0:T(8,128)(2,1)S(1)}, bf16[8,128,512]{2,1,0:T(8,128)(2,1)S(1)}) fusion(f32[128,512]{1,0:T(8,128)S(1)} %iota_multiply_fusion.5, f32[8,512]{1,0:T(8,128)S(1)} %iota_multiply_fusion.6), kind=kLoop, calls=%fused_computation.16.clone.1 | loop fusion | flops 2097152 | bytes 2375680 | tf_op jit(solution)/shard_map/convert.3
  302.0 7.7 %cosine_convert_fusion.2 = (bf16[8,128,512]{2,1,0:T(8,128)(2,1)S(1)}, bf16[8,128,512]{2,1,0:T(8,128)(2,1)S(1)}) fusion(f32[128,512]{1,0:T(8,128)S(1)} %iota_multiply_fusion.5, f32[8,512]{1,0:T(8,128)S(1)} %iota_multiply_fusion.6), kind=kLoop, calls=%fused_computation.16.clone.1 | loop fusion | flops 2097152 | bytes 2375680 | tf_op jit(solution)/shard_map/convert.3
  315.1 7.7 %cosine_convert_fusion.2 = (bf16[8,128,512]{2,1,0:T(8,128)(2,1)S(1)}, bf16[8,128,512]{2,1,0:T(8,128)(2,1)S(1)}) fusion(f32[128,512]{1,0:T(8,128)S(1)} %iota_multiply_fusion.5, f32[8,512]{1,0:T(8,128)S(1)} %iota_multiply_fusion.6), kind=kLoop, calls=%fused_computation.16.clone.1 | loop fusion | flops 2097152 | bytes 2375680 | tf_op jit(solution)/shard_map/convert.3
  328.1 7.7 %cosine_convert_fusion.2 = (bf16[8,128,512]{2,1,0:T(8,128)(2,1)S(1)}, bf16[8,128,512]{2,1,0:T(8,128)(2,1)S(1)}) fusion(f32[128,512]{1,0:T(8,128)S(1)} %iota_multiply_fusion.5, f32[8,512]{1,0:T(8,128)S(1)} %iota_multiply_fusion.6), kind=kLoop, calls=%fused_computation.16.clone.1 | loop fusion | flops 2097152 | bytes 2375680 | tf_op jit(solution)/shard_map/convert.3
  341.2 7.7 %cosine_convert_fusion.2 = (bf16[8,128,512]{2,1,0:T(8,128)(2,1)S(1)}, bf16[8,128,512]{2,1,0:T(8,128)(2,1)S(1)}) fusion(f32[128,512]{1,0:T(8,128)S(1)} %iota_multiply_fusion.5, f32[8,512]{1,0:T(8,128)S(1)} %iota_multiply_fusion.6), kind=kLoop, calls=%fused_computation.16.clone.1 | loop fusion | flops 2097152 | bytes 2375680 | tf_op jit(solution)/shard_map/convert.3
  354.2 7.7 %cosine_convert_fusion.2 = (bf16[8,128,512]{2,1,0:T(8,128)(2,1)S(1)}, bf16[8,128,512]{2,1,0:T(8,128)(2,1)S(1)}) fusion(f32[128,512]{1,0:T(8,128)S(1)} %iota_multiply_fusion.5, f32[8,512]{1,0:T(8,128)S(1)} %iota_multiply_fusion.6), kind=kLoop, calls=%fused_computation.16.clone.1 | loop fusion | flops 2097152 | bytes 2375680 | tf_op jit(solution)/shard_map/convert.3
  367.3 7.7 %cosine_convert_fusion.2 = (bf16[8,128,512]{2,1,0:T(8,128)(2,1)S(1)}, bf16[8,128,512]{2,1,0:T(8,128)(2,1)S(1)}) fusion(f32[128,512]{1,0:T(8,128)S(1)} %iota_multiply_fusion.5, f32[8,512]{1,0:T(8,128)S(1)} %iota_multiply_fusion.6), kind=kLoop, calls=%fused_computation.16.clone.1 | loop fusion | flops 2097152 | bytes 2375680 | tf_op jit(solution)/shard_map/convert.3
  380.4 7.7 %cosine_convert_fusion.2 = (bf16[8,128,512]{2,1,0:T(8,128)(2,1)S(1)}, bf16[8,128,512]{2,1,0:T(8,128)(2,1)S(1)}) fusion(f32[128,512]{1,0:T(8,128)S(1)} %iota_multiply_fusion.5, f32[8,512]{1,0:T(8,128)S(1)} %iota_multiply_fusion.6), kind=kLoop, calls=%fused_computation.16.clone.1 | loop fusion | flops 2097152 | bytes 2375680 | tf_op jit(solution)/shard_map/convert.3
  393.4 7.7 %cosine_convert_fusion.2 = (bf16[8,128,512]{2,1,0:T(8,128)(2,1)S(1)}, bf16[8,128,512]{2,1,0:T(8,128)(2,1)S(1)}) fusion(f32[128,512]{1,0:T(8,128)S(1)} %iota_multiply_fusion.5, f32[8,512]{1,0:T(8,128)S(1)} %iota_multiply_fusion.6), kind=kLoop, calls=%fused_computation.16.clone.1 | loop fusion | flops 2097152 | bytes 2375680 | tf_op jit(solution)/shard_map/convert.3
  406.5 7.7 %cosine_convert_fusion.2 = (bf16[8,128,512]{2,1,0:T(8,128)(2,1)S(1)}, bf16[8,128,512]{2,1,0:T(8,128)(2,1)S(1)}) fusion(f32[128,512]{1,0:T(8,128)S(1)} %iota_multiply_fusion.5, f32[8,512]{1,0:T(8,128)S(1)} %iota_multiply_fusion.6), kind=kLoop, calls=%fused_computation.16.clone.1 | loop fusion | flops 2097152 | bytes 2375680 | tf_op jit(solution)/shard_map/convert.3
  419.5 7.7 %cosine_convert_fusion.2 = (bf16[8,128,512]{2,1,0:T(8,128)(2,1)S(1)}, bf16[8,128,512]{2,1,0:T(8,128)(2,1)S(1)}) fusion(f32[128,512]{1,0:T(8,128)S(1)} %iota_multiply_fusion.5, f32[8,512]{1,0:T(8,128)S(1)} %iota_multiply_fusion.6), kind=kLoop, calls=%fused_computation.16.clone.1 | loop fusion | flops 2097152 | bytes 2375680 | tf_op jit(solution)/shard_map/convert.3
  430.0 1.4 slice.617
  431.5 1.0 pad_maximum_fusion.7
  432.4 141.7 %reduce-scatter.2.cloned.1.call-done = f32[256,8]{0,1:T(8,128)} async-done(((f32[8192,8]{0,1:T(8,128)}), f32[256,8]{0,1:T(8,128)}) %reduce-scatter.2.cloned.1.call-update) | async-done | bytes 8208 | tf_op jit(solution)/shard_map/reduce_scatter | solution.py:258
  (338 shorter events, 69.8 us)
Async XLA Ops:
  7.2 110.7 %copy-start = (s32[1,4]{1,0:T(1,128)S(1)}, s32[1,4]{1,0:T(1,128)}, u32[]{:S(2)}) copy-start(s32[1,4]{1,0:T(1,128)} %param.22) | copy-start | bytes 52
  7.2 2.7 copy-start.7
  7.2 3.5 copy-start.12
  7.2 566.9 %reduce-scatter.2.cloned.1.call-start = ((), (), s32[]{:S(2)}) async-start(), calls=%async_computation.1 | async-start | bytes 270336 | tf_op jit(solution)/shard_map/reduce_scatter | solution.py:258
  10.0 16.7 %copy-start.16 = (s32[1,4,18]{2,1,0:T(4,128)S(1)}, s32[1,4,18]{2,1,0:T(4,128)}, u32[]{:S(2)}) copy-start(s32[1,4,18]{2,1,0:T(4,128)} %param.23) | copy-start | bytes 868
  10.0 16.7 %copy-start.15 = (f32[2,8192]{1,0:T(2,128)S(1)}, f32[2,8192]{1,0:T(2,128)}, u32[]{:S(2)}) copy-start(f32[2,8192]{1,0:T(2,128)} %param.24) | copy-start | bytes 196612
  10.0 16.8 %copy-start.14 = (s32[8192]{0:T(1024)S(1)}, s32[8192]{0:T(1024)}, u32[]{:S(2)}) copy-start(s32[8192]{0:T(1024)} %param.25) | copy-start | bytes 98308
  19.6 100.4 %collective-permute-start.1 = (f32[16,4,16,128]{3,2,1,0:T(8,128)}, f32[16,4,16,128]{3,2,1,0:T(8,128)S(1)}, u32[]{:S(2)}, u32[]{:S(2)}) collective-permute-start(f32[16,4,16,128]{3,2,1,0:T(8,128)} %get-tuple-element.129), channel_id=1, source_target_pairs={{16,0},{17,1},{18,2},{19,3},{20,4},{21,5},{22,6},{23,7},{24,8},{25... | collective-permute-start | bytes 1572872 | tf_op jit(solution)/shard_map/ppermute | solution.py:26
  20.9 99.1 %collective-permute-start = (f32[16,4,16,128]{3,2,1,0:T(8,128)}, f32[16,4,16,128]{3,2,1,0:T(8,128)}, u32[]{:S(2)}, u32[]{:S(2)}) collective-permute-start(f32[16,4,16,128]{3,2,1,0:T(8,128)} %get-tuple-element.128), channel_id=1, source_target_pairs={{0,16},{1,17},{2,18},{3,19},{4,20},{5,21},{6,22},{7,23},{8,24},{9,... | collective-permute-start | bytes 1572872 | tf_op jit(solution)/shard_map/ppermute | solution.py:23
  120.0 1.6 copy-start.3
  121.7 6.0 %collective-permute-start.3 = (f32[16,24,4,128]{3,2,1,0:T(4,128)S(1)}, f32[16,24,4,128]{3,2,1,0:T(4,128)S(1)}, u32[]{:S(2)}, u32[]{:S(2)}) collective-permute-start(f32[16,24,4,128]{3,2,1,0:T(4,128)S(1)} %get-tuple-element.118), channel_id=1, source_target_pairs={{4,0},{8,4},{12,8},{5,1},{9,5},{13,9},{6,2},{10,6},{14,10},{7,3},{... | collective-permute-start | bytes 2359304 | tf_op jit(solution)/shard_map/ppermute | solution.py:26
  123.0 5.1 collective-permute-start.2
  140.3 15.8 %collective-permute-start.5 = (f32[16,24,24,4]{2,1,3,0:T(8,128)}, f32[16,24,24,4]{2,1,3,0:T(8,128)}, u32[]{:S(2)}, u32[]{:S(2)}) collective-permute-start(f32[16,24,24,4]{2,1,3,0:T(8,128)} %copy.52), channel_id=1, source_target_pairs={{1,0},{2,1},{3,2},{5,4},{6,5},{7,6},{9,8},{10,9},{11,10},{13,12},{... | collective-permute-start | bytes 442376 | tf_op jit(solution)/shard_map/ppermute | solution.py:26
  146.5 16.2 %collective-permute-start.4 = (f32[16,24,24,4]{2,1,3,0:T(8,128)}, f32[16,24,24,4]{2,1,3,0:T(8,128)}, u32[]{:S(2)}, u32[]{:S(2)}) collective-permute-start(f32[16,24,24,4]{2,1,3,0:T(8,128)} %copy.51), channel_id=1, source_target_pairs={{0,1},{1,2},{2,3},{4,5},{5,6},{6,7},{8,9},{9,10},{10,11},{12,13},{... | collective-permute-start | bytes 442376 | tf_op jit(solution)/shard_map/ppermute | solution.py:23
  162.7 8.3 %slice-start = ((s8[4718592]{0:T(1024)(128)(4,1)}), s8[524288]{0:T(1024)(128)(4,1)S(1)}, s32[]{:S(2)}) async-start(s8[4718592]{0:T(1024)(128)(4,1)} %bitcast.327), calls=%async_computation.2 | async-start | bytes 1048576
  167.7 3.3 slice-start.1
  167.7 4.5 copy-start.2
  167.7 4.5 copy-start.4
  174.8 1.5 copy-start.5
  206.5 1.3 copy-start.6
  207.8 7.6 %copy-start.8 = (f32[2,16,16,128]{3,2,1,0:T(8,128)S(1)}, f32[2,16,16,128]{3,2,1,0:T(8,128)}, u32[]{:S(2)}) copy-start(f32[2,16,16,128]{3,2,1,0:T(8,128)} %slice.621) | copy-start | bytes 786436
  207.8 8.8 %copy-start.9 = (f32[2,16,16,128]{3,2,1,0:T(8,128)S(1)}, f32[2,16,16,128]{3,2,1,0:T(8,128)}, u32[]{:S(2)}) copy-start(f32[2,16,16,128]{3,2,1,0:T(8,128)} %slice.620) | copy-start | bytes 786436
  212.0 5.7 copy-start.10
  212.0 5.7 copy-start.11
  219.0 1.1 copy-start.13
  429.1 145.1 %copy-start.1 = (s32[1,4]{1,0:T(1,128)S(1)}, s32[1,4]{1,0:T(1,128)}, u32[]{:S(2)}) copy-start(s32[1,4]{1,0:T(1,128)} %param.22) | copy-start | bytes 52
Sparse Core Ops, SparseCore 0:
  429.9 144.1 reduce-scatter.1
where the time goes:
time: 584 us; the launch traced here: 581 us
  other arithmetic  188 us (32%)
  local copies, waits for them, and re-layouts  171 us (29%)
  waiting for transfers between devices  147 us (25%)
  loops' own time  32.8 us (6%)
  starting transfers between devices  19.6 us (3%)
  between operations  14.7 us (3%)
  matrix products  7.61 us (1%)
    reduce_scatter x1, waiting for transfers between devices, shards(): lax.psum_scatter(far_blocks.transpose(0, 2, 1).reshape(DIRS // devices_al...  142 us
    another operation x16, other arithmetic  123 us
    gather x1, local copies, waits for them, and re-layouts, shards(): azimuth = jnp.take(dir_angles[1], dir_order)  45.5 us
    gather x1, local copies, waits for them, and re-layouts, shards(): polar_angle = jnp.take(dir_angles[0], dir_order)  45.5 us
    another operation x1, loops' own time, shards(): lax.map(block_far, jnp.arange(DIRS // devices_all * lax.axis_size(('gx',...  32.8 us
    ppermute x3, starting transfers between devices, with_halo(): lax.ppermute(lax.slice_in_dim(block, block.shape[dim] - width, None, axis...  15.8 us
    slice x16, local copies, waits for them, and re-layouts, far_block(): directions[0][None, :] * tile_x[:, None]  14.5 us
  transfers between devices with their start and end apart: 7, of which 4 were waited for; matrix products, arithmetic and copies ran while one was open for 18% of the time, Pallas kernels for 0%

commit v1 on v0

v1 whole, which is shorter than its diff:
```python
import functools
import math

import jax
import jax.numpy as jnp
from jax import lax
from jax.experimental import pallas as pl
from jax.experimental.pallas import tpu as pltpu
from jax.sharding import PartitionSpec as P

TY = 8
STEPS = 4
TILE_MEAN = 6
SPEED = 0.5
WAVE = 0.35
LANES = 128
MESH = pl.DeviceIdType.MESH

SIN_TERMS = (
    6.283185302511505, -41.34170040531808, 81.60513138582216, -76.70301535428969,
    42.02592698929055, -14.899846680245616, 3.238137526404064,
)
COS_TERMS = (
    0.9999999890590243, -19.73920449945407, 64.93911745990263, -85.45013953100009,
    60.16763095180868, -25.967599251355935, 6.528658164931359,
)


def poly(s, terms):
    total = jnp.full_like(s, terms[-1])
    for term in terms[-2::-1]:
        total = total * s + term
    return total


def cos_sin(turns):
    t = turns - jnp.round(turns)
    s = t * t
    return poly(s, COS_TERMS), t * poly(s, SIN_TERMS)


def pick(step, values):
    result = jnp.float32(values[-1])
    for index in range(len(values) - 2, -1, -1):
        result = jnp.where(step == index, jnp.float32(values[index]), result)
    return result


def kernel(
    sizes, slots, rows,
    fields_ref, pol_ref, mat_ref, omega_ref, damp_ref, strength_ref, count_ref, place_ref,
    angles_ref, order_ref,
    out_ref, far_ref,
    ele, mag, pq, coef, acc, cur, coords, dirs, table, blocks, landed,
    e_x, e_y, e_z, h_x, h_y, h_z, sx, sy, sz,
    face_send, face_recv, pair_send, pair_recv, far_send, far_recv,
):
    n_x, n_y, n_z = sizes
    half_y = n_y // 2
    owners = n_x * half_y * n_z
    width_x, width_y, depth_z = mat_ref.shape
    blocks_y = width_y // TY
    reach = rows // 2
    ix, iy, iz = lax.axis_index("gx"), lax.axis_index("gy"), lax.axis_index("gz")
    parity = lax.rem(iy, 2)
    me = (ix * half_y + iy // 2) * n_z + iz
    place_in = (("gx", ix, n_x), ("gy", iy, n_y), ("gz", iz, n_z))

    def owner_device(m):
        return {
            "gx": m // (half_y * n_z),
            "gy": lax.rem(m // n_z, half_y) * 2 + parity,
            "gz": lax.rem(m, n_z),
        }

    for ghost in (e_x, e_y, e_z, h_x, h_y, h_z):
        ghost[...] = jnp.zeros_like(ghost)

    barrier = pltpu.get_barrier_semaphore()

    def greet(o, carry):
        pl.semaphore_signal(
            barrier, inc=1, device_id=owner_device(lax.rem(me + o, owners)), device_id_type=MESH
        )
        return carry

    lax.fori_loop(1, owners, greet, 0)

    @pl.when(iy > 0)
    def _():
        pl.semaphore_signal(barrier, inc=1, device_id={"gy": iy - 1}, device_id_type=MESH)

    @pl.when(iy < n_y - 1)
    def _():
        pl.semaphore_signal(barrier, inc=1, device_id={"gy": iy + 1}, device_id_type=MESH)

    for c in range(3):
        ele[c, pl.ds(0, width_x)] = fields_ref[c]
        mag[c, pl.ds(1, width_x)] = fields_ref[3 + c]
        pq[0, c] = pol_ref[c]
        pq[1, c] = pol_ref[3 + c]
    material = mat_ref[...]
    coefs = [jnp.zeros(material.shape, jnp.float32) for _ in range(3)]
    for m in range(omega_ref.shape[0]):
        w, g, s = omega_ref[m], damp_ref[m], strength_ref[m]
        w, g, s = (jnp.full((1, 1, depth_z), v, jnp.float32) for v in (w, g, s))
        below = 1.0 + 0.5 * g
        chosen = material == m + 1
        for i, v in enumerate(((2.0 - w * w) / below, -(1.0 - 0.5 * g) / below, s * (w * w) / below)):
            coefs[i] = jnp.where(chosen, v, coefs[i])
    for i in range(3):
        coef[i] = coefs[i]
    coef[3] = jnp.where(material > 0, 1.0, 0.0).astype(jnp.float32)

    first_x, first_y, first_z = ix * width_x, iy * width_y, iz * depth_z
    lane = lax.broadcasted_iota(jnp.int32, (1, LANES), 1)
    coords[0] = jnp.zeros(coords.shape[1:], jnp.float32)
    for j in range(slots):
        p = place_ref[0, iz, j]
        x0 = (first_x + p // blocks_y).astype(jnp.float32)
        y0 = (first_y + lax.rem(p, blocks_y) * TY).astype(jnp.float32)
        z0 = first_z.astype(jnp.float32)
        live = jnp.where(j < count_ref[0, iz], jnp.float32(1.0), jnp.float32(0.0))
        row = jnp.where(lane == 0, x0, 0.0) + jnp.where(lane == 1, y0, 0.0)
        row = row + jnp.where(lane == 2, z0, 0.0) + jnp.where(lane == 3, live, 0.0)
        coords[0, j : j + 1, :] = row

    whole = angles_ref[...]
    part_a = whole.astype(jnp.bfloat16)
    left = whole - part_a.astype(jnp.float32)
    part_b = left.astype(jnp.bfloat16)
    part_c = (left - part_b.astype(jnp.float32)).astype(jnp.bfloat16)
    parts = jnp.concatenate([part_a, part_b, part_c], axis=0)
    high_count = whole.shape[1]

    pl.semaphore_wait(
        barrier,
        owners - 1 + jnp.where(iy > 0, 1, 0) + jnp.where(iy < n_y - 1, 1, 0),
    )

    per_turn = WAVE / (2.0 * math.pi)

    def build(m, carry):
        chosen = order_ref[m // n_z, parity, lax.rem(m, n_z)]
        high = lax.broadcasted_iota(jnp.int32, (high_count, reach), 0)
        low = lax.broadcasted_iota(jnp.int32, (LANES, reach), 0)
        hot = jnp.where(high == chosen // LANES, 1.0, 0.0).astype(jnp.bfloat16)
        found = jnp.dot(parts, hot, preferred_element_type=jnp.float32)
        third = 2 * LANES
        found = found[:third] + found[third : 2 * third] + found[2 * third :]
        own = low == lax.rem(chosen, LANES)
        theta = jnp.sum(jnp.where(own, found[:LANES], 0.0), axis=0, keepdims=True)
        phi = jnp.sum(jnp.where(own, found[LANES:], 0.0), axis=0, keepdims=True)
        ct, st = cos_sin(theta * (1.0 / (2.0 * math.pi)))
        cp, sp = cos_sin(phi * (1.0 / (2.0 * math.pi)))
        ux, uy, uz = st * cp * per_turn, st * sp * per_turn, ct * per_turn
        dirs[m, 0:1, :] = ux
        dirs[m, 1:2, :] = uy
        dirs[m, 2:3, :] = uz
        z_pos = lax.broadcasted_iota(jnp.int32, (depth_z, reach), 0).astype(jnp.float32)
        zc, zs = cos_sin(uz * z_pos)
        y_pos = lax.broadcasted_iota(jnp.int32, (TY, reach), 0).astype(jnp.float32)
        yc, ys = cos_sin(uy * y_pos)
        for ty in range(TY):
            c, s = yc[ty : ty + 1, :], ys[ty : ty + 1, :]
            block = pl.ds(ty * depth_z, depth_z)
            table[m, block, pl.ds(0, reach)] = (zc * c - zs * s).astype(jnp.bfloat16)
            table[m, block, pl.ds(reach, reach)] = (zc * s + zs * c).astype(jnp.bfloat16)
        return carry

    phases = 2 * STEPS
    share = -(-owners // phases)

    def build_share(phase):
        lax.fori_loop(
            jnp.minimum(phase * share, owners), jnp.minimum((phase + 1) * share, owners), build, 0
        )

    lane2 = lax.broadcasted_iota(jnp.int32, (width_y, LANES), 1)
    row2 = lax.broadcasted_iota(jnp.int32, (width_y, LANES), 0)

    def face_copies(step, kind, ghosts, toward):
        result = []
        for axis, ((name, index, count), ghost, source) in enumerate(
            zip(place_in, ghosts, (sx, sy, sz))
        ):
            copy = pltpu.make_async_remote_copy(
                src_ref=source.at[kind, step],
                dst_ref=ghost.at[step],
                send_sem=face_send.at[kind, axis],
                recv_sem=face_recv.at[step, kind, axis],
                device_id={name: index + toward},
                device_id_type=MESH,
            )
            low, high = index > 0, index < count - 1
            result.append((low, high, copy) if toward < 0 else (high, low, copy))
        return result

    def start_all(copies):
        for sends, _, copy in copies:
            pl.when(sends)(copy.start)

    def wait_all(copies):
        for sends, receives, copy in copies:
            pl.when(sends)(copy.wait_send)
            pl.when(receives)(copy.wait_recv)

    def pack_z(pairs, from_lane):
        total = jnp.zeros((width_y, LANES), jnp.float32)
        for k, plane in enumerate(pairs):
            for x in range(width_x):
                at = k * width_x + x
                rolled = pltpu.roll(plane(x), (at - from_lane) % LANES, 1)
                total = jnp.where(lane2 == at, rolled, total)
        return total

    def step_body(step, carry):
        now, old = lax.rem(step, 2), lax.rem(step + 1, 2)
        sx[0, step, 0] = ele[1, 0]
        sx[0, step, 1] = ele[2, 0]
        sy[0, step, 0] = ele[0, pl.ds(0, width_x), 0, :]
        sy[0, step, 1] = ele[2, pl.ds(0, width_x), 0, :]
        sz[0, step] = pack_z((lambda x: ele[0, x], lambda x: ele[1, x]), 0)
        copies = face_copies(step, 0, (e_x, e_y, e_z), -1)
        start_all(copies)
        build_share(2 * step)
        wait_all(copies)
        ele[1, width_x] = e_x[step, 0]
        ele[2, width_x] = e_x[step, 1]
        packed = e_z[step]
        for x in range(width_x):
            ex, ey, ez = ele[0, x], ele[1, x], ele[2, x]

            def up_y(f, k):
                return jnp.where(
                    row2 == width_y - 1, e_y[step, k, x : x + 1, :], pltpu.roll(f, width_y - 1, 0)
                )

            def up_z(f, k):
                ghost = pltpu.roll(packed, (LANES - 1 - k * width_x - x) % LANES, 1)
                return jnp.where(lane2 == LANES - 1, ghost, pltpu.roll(f, LANES - 1, 1))

            hx = mag[0, x + 1] - SPEED * ((up_y(ez, 1) - ez) - (up_z(ey, 1) - ey))
            hy = mag[1, x + 1] - SPEED * ((up_z(ex, 0) - ex) - (ele[2, x + 1] - ez))
            hz = mag[2, x + 1] - SPEED * ((ele[1, x + 1] - ey) - (up_y(ex, 0) - ex))
            mag[0, x + 1] = hx
            mag[1, x + 1] = hy
            mag[2, x + 1] = hz
        sx[1, step, 0] = mag[1, width_x]
        sx[1, step, 1] = mag[2, width_x]
        sy[1, step, 0] = mag[0, pl.ds(1, width_x), width_y - 1, :]
        sy[1, step, 1] = mag[2, pl.ds(1, width_x), width_y - 1, :]
        sz[1, step] = pack_z((lambda x: mag[0, x + 1], lambda x: mag[1, x + 1]), depth_z - 1)
        copies = face_copies(step, 1, (h_x, h_y, h_z), 1)
        start_all(copies)
        build_share(2 * step + 1)
        wait_all(copies)
        mag[1, 0] = h_x[step, 0]
        mag[2, 0] = h_x[step, 1]
        packed_h = h_z[step]
        angle = [WAVE * SPEED * (n + 0.5) for n in range(STEPS)]
        angle_e = [WAVE * SPEED * (n + 1.0) for n in range(STEPS)]
        cos_h, sin_h = pick(step, [math.cos(a) for a in angle]), pick(step, [math.sin(a) for a in angle])
        cos_e, sin_e = pick(step, [math.cos(a) for a in angle_e]), pick(step, [math.sin(a) for a in angle_e])
        for x in range(width_x):
            hx, hy, hz = mag[0, x + 1], mag[1, x + 1], mag[2, x + 1]

            def down_y(f, k):
                return jnp.where(row2 == 0, h_y[step, k, x : x + 1, :], pltpu.roll(f, 1, 0))

            def down_z(f, k):
                ghost = pltpu.roll(packed_h, (-k * width_x - x) % LANES, 1)
                return jnp.where(lane2 == 0, ghost, pltpu.roll(f, 1, 1))

            curl = (
                (hz - down_y(hz, 1)) - (hy - down_z(hy, 1)),
                (hx - down_z(hx, 0)) - (hz - mag[2, x]),
                (hy - mag[1, x]) - (hx - down_y(hx, 0)),
            )
            e = [ele[c, x] for c in range(3)]
            sat = 1.0 / (1.0 + e[0] * e[0] + e[1] * e[1] + e[2] * e[2])
            a, b, strength, sheet = coef[0, x], coef[1, x], coef[2, x] * sat, coef[3, x]
            for c in range(3):
                p = pq[now, c, x]
                pn = a * p + b * pq[old, c, x] + strength * e[c]
                pq[old, c, x] = pn
                e[c] = e[c] + SPEED * curl[c] - sheet * (pn - p)
                ele[c, x] = e[c]
            terms = (
                -cos_h * hz, sin_h * hz, cos_h * hy, -sin_h * hy,
                cos_e * e[2], -sin_e * e[2], -cos_e * e[1], sin_e * e[1],
            )
            for c, term in enumerate(terms):
                for k in range(blocks_y):
                    at = x * blocks_y + k
                    acc[c, at] = acc[c, at] + term[k * TY : (k + 1) * TY]
        return carry

    acc[...] = jnp.zeros_like(acc)
    lax.fori_loop(0, STEPS, step_body, 0)
    for c in range(3):
        out_ref[c] = ele[c, pl.ds(0, width_x)]
        out_ref[3 + c] = mag[c, pl.ds(1, width_x)]

    for j in range(0, slots, 2):
        p, q = place_ref[0, iz, j], place_ref[0, iz, min(j + 1, slots - 1)]
        for ty in range(TY):
            pair = jnp.concatenate([acc[:, p, ty, :], acc[:, q, ty, :]], axis=0)
            cur[0, pl.ds(j * 8, 16), pl.ds(ty * depth_z, depth_z)] = pair.astype(jnp.bfloat16)

    partner = {"gy": iy + 1 - 2 * parity}
    to_pair = [
        pltpu.make_async_remote_copy(
            src_ref=buffer.at[0], dst_ref=buffer.at[1],
            send_sem=pair_send.at[k], recv_sem=pair_recv.at[k],
            device_id=partner, device_id_type=MESH,
        )
        for k, buffer in enumerate((cur, coords))
    ]
    for copy in to_pair:
        copy.start()
    for copy in to_pair:
        copy.wait()

    scale = 1.0 / math.sqrt(n_x * n_y * n_z * TILE_MEAN * TY * depth_z)
    even = lax.rem(lax.broadcasted_iota(jnp.int32, (8, reach), 0), 2) == 0

    def far_copy(o):
        m = lax.rem(me + o, owners)
        return pltpu.make_async_remote_copy(
            src_ref=blocks.at[o], dst_ref=landed.at[o],
            send_sem=far_send.at[o], recv_sem=far_recv.at[o],
            device_id=owner_device(m), device_id_type=MESH,
        )

    def far_block(o):
        m = lax.rem(me + o, owners)
        ux, uy, uz = dirs[m, 0:1, :], dirs[m, 1:2, :], dirs[m, 2:3, :]
        u = jnp.zeros((8, reach), jnp.float32)
        v = jnp.zeros((8, reach), jnp.float32)
        for half in range(2):
            at = coords[half]
            tc, ts = cos_sin(at[:, 0:1] * ux + at[:, 1:2] * uy + at[:, 2:3] * uz)
            tc, ts = tc * at[:, 3:4], ts * at[:, 3:4]
            product = jnp.dot(cur[half], table[m], preferred_element_type=jnp.float32)
            for j in range(slots):
                pc = product[j * 8 : j * 8 + 8, :reach]
                ps = product[j * 8 : j * 8 + 8, reach:]
                c, s = tc[j : j + 1, :], ts[j : j + 1, :]
                u = u + (pc * c - ps * s)
                v = v + (pc * s + ps * c)
        blocks[o] = jnp.where(even, u - pltpu.roll(v, 7, 0), u + pltpu.roll(v, 1, 0)) * scale

    def far_step(o, carry):
        far_block(o)
        far_copy(o).start()
        return carry

    lax.fori_loop(1, owners, far_step, 0)
    far_block(0)

    def gather_step(o, total):
        far_copy(o).wait()
        return total + landed[o]

    total = lax.fori_loop(1, owners, gather_step, blocks[0])
    far_ref[...] = total


def shards(
    fields, polarization, material, omega0, damping, strength,
    tile_count, tile_place, dir_angles, dir_order,
):
    sizes = tuple(lax.axis_size(name) for name in ("gx", "gy", "gz"))
    n_x, n_y, n_z = sizes
    devices = n_x * n_y * n_z
    width_x, width_y, depth_z = material.shape
    slots = tile_place.shape[2]
    count = dir_order.shape[0]
    reach = count // devices
    owners = devices // 2
    angles = dir_angles.reshape(2, count // LANES, LANES).transpose(0, 2, 1)
    angles = angles.reshape(2 * LANES, count // LANES)
    order = dir_order.reshape(n_x * (n_y // 2), 2, n_z, 1, reach)
    even_slots = slots + slots % 2
    coord_rows = -(-slots // 8) * 8
    f32 = jnp.float32
    vmem, smem = pl.BlockSpec(memory_space=pltpu.VMEM), pl.BlockSpec(memory_space=pltpu.SMEM)
    x_face, y_face, z_face = (2, width_y, depth_z), (2, width_x, depth_z), (width_y, LANES)
    fields_out, far = pl.pallas_call(
        functools.partial(kernel, sizes, slots, 2 * reach),
        out_shape=(
            jax.ShapeDtypeStruct(fields.shape, f32),
            jax.ShapeDtypeStruct((8, reach), f32),
        ),
        in_specs=[vmem] * 3 + [smem] * 5 + [vmem] * 2,
        out_specs=(vmem, vmem),
        scratch_shapes=[
            pltpu.VMEM((3, width_x + 1, width_y, depth_z), f32),
            pltpu.VMEM((3, width_x + 1, width_y, depth_z), f32),
            pltpu.VMEM((2, 3, width_x, width_y, depth_z), f32),
            pltpu.VMEM((4, width_x, width_y, depth_z), f32),
            pltpu.VMEM((8, width_x * width_y // TY, TY, depth_z), f32),
            pltpu.VMEM((2, even_slots * 8, TY * depth_z), jnp.bfloat16),
            pltpu.VMEM((2, coord_rows, LANES), f32),
            pltpu.VMEM((owners, 8, reach), f32),
            pltpu.VMEM((owners, TY * depth_z, 2 * reach), jnp.bfloat16),
            pltpu.VMEM((owners, 8, reach), f32),
            pltpu.VMEM((owners, 8, reach), f32),
        ]
        + [pltpu.VMEM((STEPS,) + face, f32) for face in (x_face, y_face, z_face)] * 2
        + [pltpu.VMEM((2, STEPS) + face, f32) for face in (x_face, y_face, z_face)]
        + [
            pltpu.SemaphoreType.DMA((2, 3)),
            pltpu.SemaphoreType.DMA((STEPS, 2, 3)),
            pltpu.SemaphoreType.DMA((2,)),
            pltpu.SemaphoreType.DMA((2,)),
            pltpu.SemaphoreType.DMA((owners,)),
            pltpu.SemaphoreType.DMA((owners,)),
        ],
        compiler_params=pltpu.CompilerParams(
            collective_id=0, has_side_effects=True, vmem_limit_bytes=56 * 1024 * 1024
        ),
    )(
        fields, polarization, material, omega0, damping, strength,
        tile_count, tile_place, angles, order,
    )
    return fields_out, far.T


def solution(mesh):
    placed = (
        P(None, "gx", "gy", "gz"),
        P(None, "gx", "gy", "gz"),
        P("gx", "gy", "gz"),
        P(),
        P(),
        P(),
        P(("gx", "gy"), None),
        P(("gx", "gy"), None, None),
        P(),
        P(),
    )
    return jax.shard_map(
        shards,
        mesh=mesh,
        in_specs=placed,
        out_specs=(P(None, "gx", "gy", "gz"), P(("gx", "gy", "gz"), None)),
        check_vma=False,
    )
```

time: 584 us -> 52 us (0.09)
  other arithmetic: 188 us -> 0 us
  local copies, waits for them, and re-layouts: 171 us -> 4.31 us
  waiting for transfers between devices: 147 us -> 0 us
  Pallas kernels: 0 us -> 46.8 us
  loops' own time: 32.8 us -> 0 us
  starting transfers between devices: 19.6 us -> 0 us
  between operations: 14.7 us -> 0.65 us
  matrix products: 7.61 us -> 0 us
    reduce_scatter x1 -> x0, waiting for transfers between devices: 142 us -> none  [shards(): lax.psum_scatter(far_blocks.transpose(0, 2, 1).reshape(DIRS // devices_al...]
    another operation x43 -> x0, other arithmetic: 131 us -> none
    gather x10 -> x0, local copies, waits for them, and re-layouts: 100 us -> none  [the longest x1 45.5 us: shards(): azimuth = jnp.take(dir_angles[1], dir_order)]
    pallas_call x0 -> x1, Pallas kernels: none -> 46.8 us  [shards(): pl.pallas_call(functools.partial(kernel, sizes, slots, 2 * reach), out_sh...]
    slice x33 -> x0, local copies, waits for them, and re-layouts: 37.5 us -> none  [the longest x16 14.5 us: far_block(): directions[0][None, :] * tile_x[:, None]]
    another operation x1 -> x0, loops' own time: 32.8 us -> none  [shards(): lax.map(block_far, jnp.arange(DIRS // devices_all * lax.axis_size(('gx',...]
    mul x68 -> x0, other arithmetic: 20 us -> none  [the longest x4 9.44 us: shards(): (electric + SPEED * curl_back(magnetic) - wide_sheet * (pol_new - pol_now...]
    ppermute x6 -> x0, starting transfers between devices: 19.6 us -> none  [the longest x3 15.8 us: with_halo(): lax.ppermute(lax.slice_in_dim(block, block.shape[dim] - width, None, axis...]
  transfers between devices with their start and end apart: 7 -> 0, of which waited for: 4 -> 0; matrix products, arithmetic and copies ran while one was open for 18% -> 0% of each run, Pallas kernels for 0% -> 0%
where the time goes in v1:
time: 52 us; the launch traced here: 51.8 us
  Pallas kernels  46.8 us (90%)
  local copies, waits for them, and re-layouts  4.31 us (8%)
  between operations  0.65 us (1%)
    pallas_call x1, Pallas kernels, shards(): pl.pallas_call(functools.partial(kernel, sizes, slots, 2 * reach), out_sh...  46.8 us
    unnamed x5, local copies, waits for them, and re-layouts  3.55 us

profile of v1, /device:TPU:0, one launch (start us, length us, event | category | flops | bytes accessed | tf_op | source)
XLA Modules:
  0.0 51.8 jit_solution(11402309053649455554)
XLA Ops:
  0.6 0.8 %copy.15 = f32[1,2,64,128]{3,2,1,0:T(8,128)S(1)} copy(f32[1,2,64,128]{3,1,2,0:T(2,128)} %bitcast.11) | data formatting | bytes 131072
  1.5 0.8 %copy.12 = f32[2,64,128]{1,2,0:T(8,128)} copy(f32[2,64,128]{2,1,0:T(8,128)S(1)} %bitcast.10) | data formatting | bytes 131072 | tf_op jit(solution)/shard_map/reshape | solution.py:382
  2.2 46.8 %shard_map.113 = (f32[6,16,16,128]{3,2,1,0:T(8,128)}, f32[8,256]{1,0:T(8,128)}) custom-call(f32[6,16,16,128]{3,2,1,0:T(8,128)} %fields_ref.1, f32[6,16,16,128]{3,2,1,0:T(8,128)} %pol_ref.1, s32[16,16,128]{2,1,0:T(8,128)} %mat_ref.1, f32[4]{0:T(128)} %omega_ref.1, f32[4]{0:T(128)} %damp_ref.1, f32[4]{0:T(128)} %strength_ref.1, s32[1,4]{1,0:T(1,128)} %count_ref.1, ...), custom_call_target="tpu_custom_call" | custom-call | tf_op jit(solution)/shard_map/pallas_call | solution.py:390
  49.1 0.0 copy-start
  49.1 2.1 %copy.18 = f32[6,16,16,128]{3,2,1,0:T(8,128)} copy(f32[6,16,16,128]{3,2,1,0:T(8,128)} %get-tuple-element.8) | data formatting | bytes 1572864
  51.2 0.0 copy-done
  51.2 0.6 %copy.19 = f32[256,8]{0,1:T(8,128)} copy(f32[256,8]{0,1:T(8,128)S(1)} %bitcast.13) | data formatting | bytes 16384
Async XLA Ops:
  49.1 2.1 %copy-start = (f32[8,256]{1,0:T(8,128)S(1)}, f32[8,256]{1,0:T(8,128)}, u32[]{:S(2)}) copy-start(f32[8,256]{1,0:T(8,128)} %get-tuple-element.5) | copy-start | bytes 24580

commit v2 on v1

--- a/solution.py
+++ b/solution.py
@@ -47,11 +47,11 @@
 
 
 def kernel(
-    sizes, slots, rows,
+    sizes, slots, reach,
     fields_ref, pol_ref, mat_ref, omega_ref, damp_ref, strength_ref, count_ref, place_ref,
     angles_ref, order_ref,
     out_ref, far_ref,
-    ele, mag, pq, coef, acc, cur, coords, dirs, table, blocks, landed,
+    ele, mag, pq, coef, acc, folded, coords, spread, parts, dirs, table, blocks, landed,
     e_x, e_y, e_z, h_x, h_y, h_z, sx, sy, sz,
     face_send, face_recv, pair_send, pair_recv, far_send, far_recv,
 ):
@@ -60,7 +60,6 @@
     owners = n_x * half_y * n_z
     width_x, width_y, depth_z = mat_ref.shape
     blocks_y = width_y // TY
-    reach = rows // 2
     ix, iy, iz = lax.axis_index("gx"), lax.axis_index("gy"), lax.axis_index("gz")
     parity = lax.rem(iy, 2)
     me = (ix * half_y + iy // 2) * n_z + iz
@@ -119,53 +118,61 @@
         p = place_ref[0, iz, j]
         x0 = (first_x + p // blocks_y).astype(jnp.float32)
         y0 = (first_y + lax.rem(p, blocks_y) * TY).astype(jnp.float32)
-        z0 = first_z.astype(jnp.float32)
+        z0 = first_z.astype(jnp.float32) + 0.5 * (depth_z - 1)
         live = jnp.where(j < count_ref[0, iz], jnp.float32(1.0), jnp.float32(0.0))
-        row = jnp.where(lane == 0, x0, 0.0) + jnp.where(lane == 1, y0, 0.0)
+        row = jnp.where(lane == 0, x0, 0.0) + jnp.where(lane == 1, y0 + 0.5 * (TY - 1), 0.0)
         row = row + jnp.where(lane == 2, z0, 0.0) + jnp.where(lane == 3, live, 0.0)
         coords[0, j : j + 1, :] = row
 
-    whole = angles_ref[...]
-    part_a = whole.astype(jnp.bfloat16)
-    left = whole - part_a.astype(jnp.float32)
-    part_b = left.astype(jnp.bfloat16)
-    part_c = (left - part_b.astype(jnp.float32)).astype(jnp.bfloat16)
-    parts = jnp.concatenate([part_a, part_b, part_c], axis=0)
-    high_count = whole.shape[1]
+    high_count = spread.shape[1]
+    for a in range(2):
+        for h in range(high_count):
+            spread[a, h : h + 1, :] = angles_ref[a : a + 1, h * LANES : (h + 1) * LANES]
+        whole = spread[a]
+        part_a = whole.astype(jnp.bfloat16).astype(jnp.float32)
+        part_b = (whole - part_a).astype(jnp.bfloat16).astype(jnp.float32)
+        part_c = whole - part_a - part_b
+        parts[a] = jnp.concatenate([part_a, part_b, part_c], axis=0).T.astype(jnp.bfloat16)
 
     pl.semaphore_wait(
         barrier,
         owners - 1 + jnp.where(iy > 0, 1, 0) + jnp.where(iy < n_y - 1, 1, 0),
     )
 
+    half_z = depth_z // 2
     per_turn = WAVE / (2.0 * math.pi)
 
     def build(m, carry):
         chosen = order_ref[m // n_z, parity, lax.rem(m, n_z)]
-        high = lax.broadcasted_iota(jnp.int32, (high_count, reach), 0)
+        high = lax.rem(lax.broadcasted_iota(jnp.int32, (3 * high_count, reach), 0), high_count)
         low = lax.broadcasted_iota(jnp.int32, (LANES, reach), 0)
         hot = jnp.where(high == chosen // LANES, 1.0, 0.0).astype(jnp.bfloat16)
-        found = jnp.dot(parts, hot, preferred_element_type=jnp.float32)
-        third = 2 * LANES
-        found = found[:third] + found[third : 2 * third] + found[2 * third :]
         own = low == lax.rem(chosen, LANES)
-        theta = jnp.sum(jnp.where(own, found[:LANES], 0.0), axis=0, keepdims=True)
-        phi = jnp.sum(jnp.where(own, found[LANES:], 0.0), axis=0, keepdims=True)
+        theta, phi = (
+            jnp.sum(
+                jnp.where(own, jnp.dot(parts[a], hot, preferred_element_type=jnp.float32), 0.0),
+                axis=0,
+                keepdims=True,
+            )
+            for a in range(2)
+        )
         ct, st = cos_sin(theta * (1.0 / (2.0 * math.pi)))
         cp, sp = cos_sin(phi * (1.0 / (2.0 * math.pi)))
         ux, uy, uz = st * cp * per_turn, st * sp * per_turn, ct * per_turn
         dirs[m, 0:1, :] = ux
         dirs[m, 1:2, :] = uy
         dirs[m, 2:3, :] = uz
-        z_pos = lax.broadcasted_iota(jnp.int32, (depth_z, reach), 0).astype(jnp.float32)
+        z_pos = lax.broadcasted_iota(jnp.int32, (half_z, reach), 0).astype(jnp.float32) + 0.5
         zc, zs = cos_sin(uz * z_pos)
-        y_pos = lax.broadcasted_iota(jnp.int32, (TY, reach), 0).astype(jnp.float32)
+        y_pos = lax.broadcasted_iota(jnp.int32, (8, reach), 0).astype(jnp.float32) + 0.5
         yc, ys = cos_sin(uy * y_pos)
-        for ty in range(TY):
-            c, s = yc[ty : ty + 1, :], ys[ty : ty + 1, :]
-            block = pl.ds(ty * depth_z, depth_z)
-            table[m, block, pl.ds(0, reach)] = (zc * c - zs * s).astype(jnp.bfloat16)
-            table[m, block, pl.ds(reach, reach)] = (zc * s + zs * c).astype(jnp.bfloat16)
+        for k in range(TY // 2):
+            c, s = yc[k : k + 1, :], ys[k : k + 1, :]
+            upper, lower = pl.ds(k * depth_z, half_z), pl.ds(k * depth_z + half_z, half_z)
+            table[m, 0, upper, :] = (zc * c).astype(jnp.bfloat16)
+            table[m, 0, lower, :] = (zs * -s).astype(jnp.bfloat16)
+            table[m, 1, upper, :] = (zc * s).astype(jnp.bfloat16)
+            table[m, 1, lower, :] = (zs * c).astype(jnp.bfloat16)
         return carry
 
     phases = 2 * STEPS
@@ -214,6 +221,20 @@
                 total = jnp.where(lane2 == at, rolled, total)
         return total
 
+    def add_phasors(x, first, terms):
+        for c, term in enumerate(terms):
+            for k in range(blocks_y):
+                at = x * blocks_y + k
+                acc[first + c, at] = acc[first + c, at] + term[k * TY : (k + 1) * TY]
+
+    def add_electric(cos_e, sin_e):
+        for x in range(width_x):
+            ey, ez = ele[1, x], ele[2, x]
+            add_phasors(x, 4, (cos_e * ez, -sin_e * ez, -cos_e * ey, sin_e * ey))
+
+    angle_h = [WAVE * SPEED * (n + 0.5) for n in range(STEPS)]
+    angle_e = [WAVE * SPEED * (n + 1.0) for n in range(STEPS)]
+
     def step_body(step, carry):
         now, old = lax.rem(step, 2), lax.rem(step + 1, 2)
         sx[0, step, 0] = ele[1, 0]
@@ -224,6 +245,10 @@
         copies = face_copies(step, 0, (e_x, e_y, e_z), -1)
         start_all(copies)
         build_share(2 * step)
+        add_electric(
+            pick(step, [0.0] + [math.cos(a) for a in angle_e[:-1]]),
+            pick(step, [0.0] + [math.sin(a) for a in angle_e[:-1]]),
+        )
         wait_all(copies)
         ele[1, width_x] = e_x[step, 0]
         ele[2, width_x] = e_x[step, 1]
@@ -254,29 +279,9 @@
         copies = face_copies(step, 1, (h_x, h_y, h_z), 1)
         start_all(copies)
         build_share(2 * step + 1)
-        wait_all(copies)
-        mag[1, 0] = h_x[step, 0]
-        mag[2, 0] = h_x[step, 1]
-        packed_h = h_z[step]
-        angle = [WAVE * SPEED * (n + 0.5) for n in range(STEPS)]
-        angle_e = [WAVE * SPEED * (n + 1.0) for n in range(STEPS)]
-        cos_h, sin_h = pick(step, [math.cos(a) for a in angle]), pick(step, [math.sin(a) for a in angle])
-        cos_e, sin_e = pick(step, [math.cos(a) for a in angle_e]), pick(step, [math.sin(a) for a in angle_e])
+        cos_h = pick(step, [math.cos(a) for a in angle_h])
+        sin_h = pick(step, [math.sin(a) for a in angle_h])
         for x in range(width_x):
-            hx, hy, hz = mag[0, x + 1], mag[1, x + 1], mag[2, x + 1]
-
-            def down_y(f, k):
-                return jnp.where(row2 == 0, h_y[step, k, x : x + 1, :], pltpu.roll(f, 1, 0))
-
-            def down_z(f, k):
-                ghost = pltpu.roll(packed_h, (-k * width_x - x) % LANES, 1)
-                return jnp.where(lane2 == 0, ghost, pltpu.roll(f, 1, 1))
-
-            curl = (
-                (hz - down_y(hz, 1)) - (hy - down_z(hy, 1)),
-                (hx - down_z(hx, 0)) - (hz - mag[2, x]),
-                (hy - mag[1, x]) - (hx - down_y(hx, 0)),
-            )
             e = [ele[c, x] for c in range(3)]
             sat = 1.0 / (1.0 + e[0] * e[0] + e[1] * e[1] + e[2] * e[2])
             a, b, strength, sheet = coef[0, x], coef[1, x], coef[2, x] * sat, coef[3, x]
@@ -284,43 +289,74 @@
                 p = pq[now, c, x]
                 pn = a * p + b * pq[old, c, x] + strength * e[c]
                 pq[old, c, x] = pn
-                e[c] = e[c] + SPEED * curl[c] - sheet * (pn - p)
-                ele[c, x] = e[c]
-            terms = (
-                -cos_h * hz, sin_h * hz, cos_h * hy, -sin_h * hy,
-                cos_e * e[2], -sin_e * e[2], -cos_e * e[1], sin_e * e[1],
+                ele[c, x] = e[c] - sheet * (pn - p)
+            hy, hz = mag[1, x + 1], mag[2, x + 1]
+            add_phasors(x, 0, (-cos_h * hz, sin_h * hz, cos_h * hy, -sin_h * hy))
+        wait_all(copies)
+        mag[1, 0] = h_x[step, 0]
+        mag[2, 0] = h_x[step, 1]
+        packed_h = h_z[step]
+        for x in range(width_x):
+            hx, hy, hz = mag[0, x + 1], mag[1, x + 1], mag[2, x + 1]
+
+            def down_y(f, k):
+                return jnp.where(row2 == 0, h_y[step, k, x : x + 1, :], pltpu.roll(f, 1, 0))
+
+            def down_z(f, k):
+                ghost = pltpu.roll(packed_h, (-k * width_x - x) % LANES, 1)
+                return jnp.where(lane2 == 0, ghost, pltpu.roll(f, 1, 1))
+
+            curl = (
+                (hz - down_y(hz, 1)) - (hy - down_z(hy, 1)),
+                (hx - down_z(hx, 0)) - (hz - mag[2, x]),
+                (hy - mag[1, x]) - (hx - down_y(hx, 0)),
             )
-            for c, term in enumerate(terms):
-                for k in range(blocks_y):
-                    at = x * blocks_y + k
-                    acc[c, at] = acc[c, at] + term[k * TY : (k + 1) * TY]
+            for c in range(3):
+                ele[c, x] = ele[c, x] + SPEED * curl[c]
         return carry
 
     acc[...] = jnp.zeros_like(acc)
     lax.fori_loop(0, STEPS, step_body, 0)
+    add_electric(math.cos(angle_e[-1]), math.sin(angle_e[-1]))
+
+    row_z = lax.broadcasted_iota(jnp.int32, (depth_z, depth_z), 0)
+    col_z = lax.broadcasted_iota(jnp.int32, (depth_z, depth_z), 1)
+    offset = lax.rem(col_z, half_z)
+    mirror = jnp.where(col_z < half_z, 1.0, -1.0)
+    fold = jnp.where(row_z == half_z + offset, 1.0, 0.0)
+    fold = (fold + jnp.where(row_z == half_z - 1 - offset, mirror, 0.0)).astype(jnp.bfloat16)
+    height = folded.shape[1] // 2
+    places = [place_ref[0, iz, min(j, slots - 1)] for j in range(height // 8)]
+    split = []
+    for ty in range(TY):
+        rows_ty = jnp.concatenate([acc[:, p, ty, :] for p in places], axis=0).astype(jnp.bfloat16)
+        split.append(jnp.dot(rows_ty, fold, preferred_element_type=jnp.float32))
+    first_half = lax.broadcasted_iota(jnp.int32, (height, depth_z), 1) < half_z
+    for k in range(TY // 2):
+        above, under = split[TY // 2 + k], split[TY // 2 - 1 - k]
+        same, other = above + under, above - under
+        block = pl.ds(k * depth_z, depth_z)
+        folded[0, pl.ds(0, height), block] = jnp.where(first_half, same, other).astype(jnp.bfloat16)
+        folded[1, pl.ds(0, height), block] = jnp.where(first_half, other, same).astype(jnp.bfloat16)
+
+    partner = {"gy": iy + 1 - 2 * parity}
+    to_pair = [
+        pltpu.make_async_remote_copy(
+            src_ref=source, dst_ref=target,
+            send_sem=pair_send.at[k], recv_sem=pair_recv.at[k],
+            device_id=partner, device_id_type=MESH,
+        )
+        for k, (source, target) in enumerate((
+            (folded.at[0, pl.ds(0, height)], folded.at[0, pl.ds(height, height)]),
+            (folded.at[1, pl.ds(0, height)], folded.at[1, pl.ds(height, height)]),
+            (coords.at[0], coords.at[1]),
+        ))
+    ]
+    for copy in to_pair:
+        copy.start()
     for c in range(3):
         out_ref[c] = ele[c, pl.ds(0, width_x)]
         out_ref[3 + c] = mag[c, pl.ds(1, width_x)]
-
-    for j in range(0, slots, 2):
-        p, q = place_ref[0, iz, j], place_ref[0, iz, min(j + 1, slots - 1)]
-        for ty in range(TY):
-            pair = jnp.concatenate([acc[:, p, ty, :], acc[:, q, ty, :]], axis=0)
-            cur[0, pl.ds(j * 8, 16), pl.ds(ty * depth_z, depth_z)] = pair.astype(jnp.bfloat16)
-
-    partner = {"gy": iy + 1 - 2 * parity}
-    to_pair = [
-        pltpu.make_async_remote_copy(
-            src_ref=buffer.at[0], dst_ref=buffer.at[1],
-            send_sem=pair_send.at[k], recv_sem=pair_recv.at[k],
-            device_id=partner, device_id_type=MESH,
-        )
-        for k, buffer in enumerate((cur, coords))
-    ]
-    for copy in to_pair:
-        copy.start()
-    for copy in to_pair:
-        copy.wait()
 
     scale = 1.0 / math.sqrt(n_x * n_y * n_z * TILE_MEAN * TY * depth_z)
     even = lax.rem(lax.broadcasted_iota(jnp.int32, (8, reach), 0), 2) == 0
@@ -333,31 +369,40 @@
             device_id=owner_device(m), device_id_type=MESH,
         )
 
-    def far_block(o):
-        m = lax.rem(me + o, owners)
+    def add_tiles(sums, m, first, halves):
+        u, v = sums
         ux, uy, uz = dirs[m, 0:1, :], dirs[m, 1:2, :], dirs[m, 2:3, :]
-        u = jnp.zeros((8, reach), jnp.float32)
-        v = jnp.zeros((8, reach), jnp.float32)
-        for half in range(2):
-            at = coords[half]
+        part = pl.ds(first * height, halves * height)
+        in_cos = jnp.dot(folded[0, part], table[m, 0], preferred_element_type=jnp.float32)
+        in_sin = jnp.dot(folded[1, part], table[m, 1], preferred_element_type=jnp.float32)
+        for half in range(halves):
+            at = coords[first + half]
             tc, ts = cos_sin(at[:, 0:1] * ux + at[:, 1:2] * uy + at[:, 2:3] * uz)
             tc, ts = tc * at[:, 3:4], ts * at[:, 3:4]
-            product = jnp.dot(cur[half], table[m], preferred_element_type=jnp.float32)
             for j in range(slots):
-                pc = product[j * 8 : j * 8 + 8, :reach]
-                ps = product[j * 8 : j * 8 + 8, reach:]
+                row = half * height + j * 8
+                pc, ps = in_cos[row : row + 8], in_sin[row : row + 8]
                 c, s = tc[j : j + 1, :], ts[j : j + 1, :]
                 u = u + (pc * c - ps * s)
                 v = v + (pc * s + ps * c)
+        return u, v
+
+    empty = (jnp.zeros((8, reach), jnp.float32), jnp.zeros((8, reach), jnp.float32))
+
+    def keep_block(o, sums):
+        u, v = sums
         blocks[o] = jnp.where(even, u - pltpu.roll(v, 7, 0), u + pltpu.roll(v, 1, 0)) * scale
 
     def far_step(o, carry):
-        far_block(o)
+        keep_block(o, add_tiles(empty, lax.rem(me + o, owners), 0, 2))
         far_copy(o).start()
         return carry
 
+    sums = add_tiles(empty, me, 0, 1)
+    for copy in to_pair:
+        copy.wait()
     lax.fori_loop(1, owners, far_step, 0)
-    far_block(0)
+    keep_block(0, add_tiles(sums, me, 1, 1))
 
     def gather_step(o, total):
         far_copy(o).wait()
@@ -379,8 +424,6 @@
     count = dir_order.shape[0]
     reach = count // devices
     owners = devices // 2
-    angles = dir_angles.reshape(2, count // LANES, LANES).transpose(0, 2, 1)
-    angles = angles.reshape(2 * LANES, count // LANES)
     order = dir_order.reshape(n_x * (n_y // 2), 2, n_z, 1, reach)
     even_slots = slots + slots % 2
     coord_rows = -(-slots // 8) * 8
@@ -388,7 +431,7 @@
     vmem, smem = pl.BlockSpec(memory_space=pltpu.VMEM), pl.BlockSpec(memory_space=pltpu.SMEM)
     x_face, y_face, z_face = (2, width_y, depth_z), (2, width_x, depth_z), (width_y, LANES)
     fields_out, far = pl.pallas_call(
-        functools.partial(kernel, sizes, slots, 2 * reach),
+        functools.partial(kernel, sizes, slots, reach),
         out_shape=(
             jax.ShapeDtypeStruct(fields.shape, f32),
             jax.ShapeDtypeStruct((8, reach), f32),
@@ -401,10 +444,12 @@
             pltpu.VMEM((2, 3, width_x, width_y, depth_z), f32),
             pltpu.VMEM((4, width_x, width_y, depth_z), f32),
             pltpu.VMEM((8, width_x * width_y // TY, TY, depth_z), f32),
-            pltpu.VMEM((2, even_slots * 8, TY * depth_z), jnp.bfloat16),
+            pltpu.VMEM((2, 2 * even_slots * 8, TY // 2 * depth_z), jnp.bfloat16),
             pltpu.VMEM((2, coord_rows, LANES), f32),
+            pltpu.VMEM((2, count // LANES, LANES), f32),
+            pltpu.VMEM((2, LANES, 3 * (count // LANES)), jnp.bfloat16),
             pltpu.VMEM((owners, 8, reach), f32),
-            pltpu.VMEM((owners, TY * depth_z, 2 * reach), jnp.bfloat16),
+            pltpu.VMEM((owners, 2, TY // 2 * depth_z, reach), jnp.bfloat16),
             pltpu.VMEM((owners, 8, reach), f32),
             pltpu.VMEM((owners, 8, reach), f32),
         ]
@@ -413,8 +458,8 @@
         + [
             pltpu.SemaphoreType.DMA((2, 3)),
             pltpu.SemaphoreType.DMA((STEPS, 2, 3)),
-            pltpu.SemaphoreType.DMA((2,)),
-            pltpu.SemaphoreType.DMA((2,)),
+            pltpu.SemaphoreType.DMA((3,)),
+            pltpu.SemaphoreType.DMA((3,)),
             pltpu.SemaphoreType.DMA((owners,)),
             pltpu.SemaphoreType.DMA((owners,)),
         ],
@@ -423,7 +468,7 @@
         ),
     )(
         fields, polarization, material, omega0, damping, strength,
-        tile_count, tile_place, angles, order,
+        tile_count, tile_place, dir_angles, order,
     )
     return fields_out, far.T
 

time: 52 us -> 47.5 us (0.913)
  Pallas kernels: 46.8 us -> 44 us
  local copies, waits for them, and re-layouts: 4.31 us -> 2.7 us
    pallas_call x1, Pallas kernels: 46.8 us -> 44 us  [shards(): pl.pallas_call(functools.partial(kernel, sizes, slots, reach), out_shape=...]
    unnamed x5 -> x4, local copies, waits for them, and re-layouts: 3.55 us -> 2.7 us
    reshape x1 -> x0, local copies, waits for them, and re-layouts: 0.76 us -> none  [shards(): angles = dir_angles.reshape(2, count // LANES, LANES).transpose(0, 2, 1)]
where the time goes in v2:
time: 47.5 us; the launch traced here: 47.4 us
  Pallas kernels  44 us (93%)
  local copies, waits for them, and re-layouts  2.7 us (6%)
  between operations  0.65 us (1%)
    pallas_call x1, Pallas kernels, shards(): pl.pallas_call(functools.partial(kernel, sizes, slots, reach), out_shape=...  44 us
    unnamed x4, local copies, waits for them, and re-layouts  2.7 us

profile of v2, /device:TPU:0, one launch (start us, length us, event | category | flops | bytes accessed | tf_op | source)
XLA Modules:
  0.0 47.4 jit_solution(18060032038827791154)
XLA Ops:
  0.6 44.0 %shard_map.113 = (f32[6,16,16,128]{3,2,1,0:T(8,128)}, f32[8,256]{1,0:T(8,128)}) custom-call(f32[6,16,16,128]{3,2,1,0:T(8,128)} %fields_ref.1, f32[6,16,16,128]{3,2,1,0:T(8,128)} %pol_ref.1, s32[16,16,128]{2,1,0:T(8,128)} %mat_ref.1, f32[4]{0:T(128)} %omega_ref.1, f32[4]{0:T(128)} %damp_ref.1, f32[4]{0:T(128)} %strength_ref.1, s32[1,4]{1,0:T(1,128)} %count_ref.1, ...), custom_call_target="tpu_custom_call" | custom-call | tf_op jit(solution)/shard_map/pallas_call | solution.py:433
  44.7 0.0 copy-start
  44.7 2.1 %copy.14 = f32[6,16,16,128]{3,2,1,0:T(8,128)} copy(f32[6,16,16,128]{3,2,1,0:T(8,128)} %get-tuple-element.8) | data formatting | bytes 1572864
  46.8 0.0 copy-done
  46.8 0.6 %copy.15 = f32[256,8]{0,1:T(8,128)} copy(f32[256,8]{0,1:T(8,128)S(1)} %bitcast.3) | data formatting | bytes 16384
Async XLA Ops:
  44.7 2.1 %copy-start = (f32[8,256]{1,0:T(8,128)S(1)}, f32[8,256]{1,0:T(8,128)}, u32[]{:S(2)}) copy-start(f32[8,256]{1,0:T(8,128)} %get-tuple-element.5) | copy-start | bytes 24580

commit v3 on v2

--- a/solution.py
+++ b/solution.py
@@ -52,7 +52,7 @@
     angles_ref, order_ref,
     out_ref, far_ref,
     ele, mag, pq, coef, acc, folded, coords, spread, parts, dirs, table, blocks, landed,
-    e_x, e_y, e_z, h_x, h_y, h_z, sx, sy, sz,
+    e_x, e_y, e_z, h_x, h_y, h_z, edge, sx, sy, sz, edge_out,
     face_send, face_recv, pair_send, pair_recv, far_send, far_recv,
 ):
     n_x, n_y, n_z = sizes
@@ -72,7 +72,7 @@
             "gz": lax.rem(m, n_z),
         }
 
-    for ghost in (e_x, e_y, e_z, h_x, h_y, h_z):
+    for ghost in (e_x, e_y, e_z, h_x, h_y, h_z, edge, edge_out):
         ghost[...] = jnp.zeros_like(ghost)
 
     barrier = pltpu.get_barrier_semaphore()
@@ -85,13 +85,24 @@
 
     lax.fori_loop(1, owners, greet, 0)
 
-    @pl.when(iy > 0)
-    def _():
-        pl.semaphore_signal(barrier, inc=1, device_id={"gy": iy - 1}, device_id_type=MESH)
-
-    @pl.when(iy < n_y - 1)
-    def _():
-        pl.semaphore_signal(barrier, inc=1, device_id={"gy": iy + 1}, device_id_type=MESH)
+    def exists(offset):
+        found = jnp.int32(1)
+        for (_, index, count), move in zip(place_in, offset):
+            if move:
+                found = found * jnp.where((index + move >= 0) & (index + move < count), 1, 0)
+        return found
+
+    def device_at(offset):
+        return {name: index + move for (name, index, _), move in zip(place_in, offset) if move}
+
+    others = ((0, 1, 0), (0, -1, 0), (1, -1, 0), (-1, 1, 0), (0, 1, -1), (0, -1, 1))
+    for offset in others:
+        pl.when(exists(offset) > 0)(
+            functools.partial(
+                pl.semaphore_signal,
+                barrier, inc=1, device_id=device_at(offset), device_id_type=MESH,
+            )
+        )
 
     for c in range(3):
         ele[c, pl.ds(0, width_x)] = fields_ref[c]
@@ -136,7 +147,7 @@
 
     pl.semaphore_wait(
         barrier,
-        owners - 1 + jnp.where(iy > 0, 1, 0) + jnp.where(iy < n_y - 1, 1, 0),
+        owners - 1 + sum(exists(offset) for offset in others),
     )
 
     half_z = depth_z // 2
@@ -175,7 +186,7 @@
             table[m, 1, lower, :] = (zs * c).astype(jnp.bfloat16)
         return carry
 
-    phases = 2 * STEPS
+    phases = STEPS
     share = -(-owners // phases)
 
     def build_share(phase):
@@ -185,22 +196,32 @@
 
     lane2 = lax.broadcasted_iota(jnp.int32, (width_y, LANES), 1)
     row2 = lax.broadcasted_iota(jnp.int32, (width_y, LANES), 0)
-
-    def face_copies(step, kind, ghosts, toward):
+    lane3 = lax.broadcasted_iota(jnp.int32, (width_x, LANES), 1)
+    row3 = lax.broadcasted_iota(jnp.int32, (width_x, LANES), 0)
+
+    def copies_of(step, group):
+        low = ((-1, 0, 0), (0, -1, 0), (0, 0, -1))
+        high = ((1, 0, 0), (0, 1, 0), (0, 0, 1))
+        across = ((1, 0, -1), (1, -1, 0), (0, 1, -1), (-1, 1, 0), (0, -1, 1), (-1, 0, 1))
+        if group == 0:
+            ends = [(s.at[0, step], d.at[step]) for s, d in zip((sx, sy, sz), (e_x, e_y, e_z))]
+            moves = list(zip(low, ends))
+            ends = [(edge_out.at[step, k], edge.at[step, k]) for k in range(6)]
+            moves = moves + list(zip(across, ends))
+        else:
+            ends = [(s.at[1, step], d.at[step]) for s, d in zip((sx, sy, sz), (h_x, h_y, h_z))]
+            moves = list(zip(high, ends))
         result = []
-        for axis, ((name, index, count), ghost, source) in enumerate(
-            zip(place_in, ghosts, (sx, sy, sz))
-        ):
+        for k, (offset, (source, target)) in enumerate(moves):
             copy = pltpu.make_async_remote_copy(
-                src_ref=source.at[kind, step],
-                dst_ref=ghost.at[step],
-                send_sem=face_send.at[kind, axis],
-                recv_sem=face_recv.at[step, kind, axis],
-                device_id={name: index + toward},
+                src_ref=source,
+                dst_ref=target,
+                send_sem=face_send.at[group * 9 + k],
+                recv_sem=face_recv.at[step, group * 9 + k],
+                device_id=device_at(offset),
                 device_id_type=MESH,
             )
-            low, high = index > 0, index < count - 1
-            result.append((low, high, copy) if toward < 0 else (high, low, copy))
+            result.append((exists(offset) > 0, exists(tuple(-m for m in offset)) > 0, copy))
         return result
 
     def start_all(copies):
@@ -242,45 +263,44 @@
         sy[0, step, 0] = ele[0, pl.ds(0, width_x), 0, :]
         sy[0, step, 1] = ele[2, pl.ds(0, width_x), 0, :]
         sz[0, step] = pack_z((lambda x: ele[0, x], lambda x: ele[1, x]), 0)
-        copies = face_copies(step, 0, (e_x, e_y, e_z), -1)
-        start_all(copies)
-        build_share(2 * step)
+        last_x, last_y, last_z = width_x - 1, width_y - 1, depth_z - 1
+        edge_out[step, 0, pl.ds(0, width_y)] = pltpu.roll(ele[0, last_x], last_z, 1)
+        edge_out[step, 1, 0:1] = ele[0, last_x, 0:1, :]
+        edge_out[step, 2, pl.ds(0, width_x)] = pltpu.roll(ele[1, pl.ds(0, width_x), last_y, :], last_z, 1)
+        edge_out[step, 3, 0:1] = ele[1, 0, last_y : last_y + 1, :]
+        edge_out[step, 4, 0:1] = pack_z((lambda x: ele[2, x],), last_z)[0:1]
+        at = 2 * width_x - 1
+        edge_out[step, 5, pl.ds(0, width_y)] = pltpu.roll(ele[2, 0], (at - last_z) % LANES, 1)
+        electric_copies = copies_of(step, 0)
+        start_all(electric_copies)
+
+        for x in range(width_x):
+            ex, ey, ez = ele[0, x], ele[1, x], ele[2, x]
+
+            def up_y(f):
+                return jnp.where(row2 == last_y, 0.0, pltpu.roll(f, last_y, 0))
+
+            def up_z(f):
+                return jnp.where(lane2 == last_z, 0.0, pltpu.roll(f, last_z, 1))
+
+            ahead_y = ele[1, x + 1] if x < last_x else jnp.zeros_like(ey)
+            ahead_z = ele[2, x + 1] if x < last_x else jnp.zeros_like(ez)
+            mag[0, x + 1] = mag[0, x + 1] - SPEED * ((up_y(ez) - ez) - (up_z(ey) - ey))
+            mag[1, x + 1] = mag[1, x + 1] - SPEED * ((up_z(ex) - ex) - (ahead_z - ez))
+            mag[2, x + 1] = mag[2, x + 1] - SPEED * ((ahead_y - ey) - (up_y(ex) - ex))
+        sx[1, step, 0] = mag[1, width_x]
+        sx[1, step, 1] = mag[2, width_x]
+        sy[1, step, 0] = mag[0, pl.ds(1, width_x), last_y, :]
+        sy[1, step, 1] = mag[2, pl.ds(1, width_x), last_y, :]
+        sz[1, step] = pack_z((lambda x: mag[0, x + 1], lambda x: mag[1, x + 1]), last_z)
+        magnetic_copies = copies_of(step, 1)
+        start_all(magnetic_copies)
+
+        build_share(step)
         add_electric(
             pick(step, [0.0] + [math.cos(a) for a in angle_e[:-1]]),
             pick(step, [0.0] + [math.sin(a) for a in angle_e[:-1]]),
         )
-        wait_all(copies)
-        ele[1, width_x] = e_x[step, 0]
-        ele[2, width_x] = e_x[step, 1]
-        packed = e_z[step]
-        for x in range(width_x):
-            ex, ey, ez = ele[0, x], ele[1, x], ele[2, x]
-
-            def up_y(f, k):
-                return jnp.where(
-                    row2 == width_y - 1, e_y[step, k, x : x + 1, :], pltpu.roll(f, width_y - 1, 0)
-                )
-
-            def up_z(f, k):
-                ghost = pltpu.roll(packed, (LANES - 1 - k * width_x - x) % LANES, 1)
-                return jnp.where(lane2 == LANES - 1, ghost, pltpu.roll(f, LANES - 1, 1))
-
-            hx = mag[0, x + 1] - SPEED * ((up_y(ez, 1) - ez) - (up_z(ey, 1) - ey))
-            hy = mag[1, x + 1] - SPEED * ((up_z(ex, 0) - ex) - (ele[2, x + 1] - ez))
-            hz = mag[2, x + 1] - SPEED * ((ele[1, x + 1] - ey) - (up_y(ex, 0) - ex))
-            mag[0, x + 1] = hx
-            mag[1, x + 1] = hy
-            mag[2, x + 1] = hz
-        sx[1, step, 0] = mag[1, width_x]
-        sx[1, step, 1] = mag[2, width_x]
-        sy[1, step, 0] = mag[0, pl.ds(1, width_x), width_y - 1, :]
-        sy[1, step, 1] = mag[2, pl.ds(1, width_x), width_y - 1, :]
-        sz[1, step] = pack_z((lambda x: mag[0, x + 1], lambda x: mag[1, x + 1]), depth_z - 1)
-        copies = face_copies(step, 1, (h_x, h_y, h_z), 1)
-        start_all(copies)
-        build_share(2 * step + 1)
-        cos_h = pick(step, [math.cos(a) for a in angle_h])
-        sin_h = pick(step, [math.sin(a) for a in angle_h])
         for x in range(width_x):
             e = [ele[c, x] for c in range(3)]
             sat = 1.0 / (1.0 + e[0] * e[0] + e[1] * e[1] + e[2] * e[2])
@@ -290,20 +310,58 @@
                 pn = a * p + b * pq[old, c, x] + strength * e[c]
                 pq[old, c, x] = pn
                 ele[c, x] = e[c] - sheet * (pn - p)
-            hy, hz = mag[1, x + 1], mag[2, x + 1]
-            add_phasors(x, 0, (-cos_h * hz, sin_h * hz, cos_h * hy, -sin_h * hy))
-        wait_all(copies)
-        mag[1, 0] = h_x[step, 0]
-        mag[2, 0] = h_x[step, 1]
-        packed_h = h_z[step]
+        wait_all(electric_copies)
+        wait_all(magnetic_copies)
+
+        in_x, in_y, in_z = (
+            jnp.where(index > 0, jnp.float32(SPEED), jnp.float32(0.0)) for _, index, _ in place_in
+        )
+        edges = [edge[step, k] for k in range(6)]
+
+        def only(condition, value):
+            return jnp.where(condition, value, 0.0)
+
+        mag[1, 0] = h_x[step, 0] + in_x * (
+            sx[0, step, 1] - only(lane2 == last_z, edges[0][:width_y])
+        )
+        mag[2, 0] = h_x[step, 1] - in_x * (sx[0, step, 0] - only(row2 == last_y, edges[1][0:1]))
+        below_y = (
+            h_y[step, 0] - in_y * (sy[0, step, 1] - only(lane3 == last_z, edges[2][:width_x])),
+            h_y[step, 1] + in_y * (sy[0, step, 0] - only(row3 == last_x, edges[3][0:1])),
+        )
+        own = sz[0, step]
+        for_x = only(lane2 < width_x, pltpu.roll(own, LANES - width_x, 1))
+        for_x = for_x - only((row2 == last_y) & (lane2 < width_x), edges[4][0:1])
+        for_y = only((lane2 >= width_x) & (lane2 < 2 * width_x), pltpu.roll(own, width_x, 1))
+        for_y = for_y - only(lane2 == at, edges[5][:width_y])
+        below_z = h_z[step] + in_z * (for_x - for_y)
+        above_z = e_z[step]
+
+        cos_h = pick(step, [math.cos(a) for a in angle_h])
+        sin_h = pick(step, [math.sin(a) for a in angle_h])
         for x in range(width_x):
-            hx, hy, hz = mag[0, x + 1], mag[1, x + 1], mag[2, x + 1]
+            def beyond_y(k):
+                return only(row2 == last_y, SPEED * e_y[step, k, x : x + 1, :])
+
+            def beyond_z(k):
+                ghost = pltpu.roll(above_z, (LANES - 1 - k * width_x - x) % LANES, 1)
+                return only(lane2 == last_z, SPEED * ghost)
+
+            hx = mag[0, x + 1] - beyond_y(1) + beyond_z(1)
+            hy = mag[1, x + 1] - beyond_z(0)
+            hz = mag[2, x + 1] + beyond_y(0)
+            if x == last_x:
+                hy = hy + SPEED * e_x[step, 1]
+                hz = hz - SPEED * e_x[step, 0]
+            mag[0, x + 1] = hx
+            mag[1, x + 1] = hy
+            mag[2, x + 1] = hz
 
             def down_y(f, k):
-                return jnp.where(row2 == 0, h_y[step, k, x : x + 1, :], pltpu.roll(f, 1, 0))
+                return jnp.where(row2 == 0, below_y[k][x : x + 1, :], pltpu.roll(f, 1, 0))
 
             def down_z(f, k):
-                ghost = pltpu.roll(packed_h, (-k * width_x - x) % LANES, 1)
+                ghost = pltpu.roll(below_z, (-k * width_x - x) % LANES, 1)
                 return jnp.where(lane2 == 0, ghost, pltpu.roll(f, 1, 1))
 
             curl = (
@@ -313,6 +371,7 @@
             )
             for c in range(3):
                 ele[c, x] = ele[c, x] + SPEED * curl[c]
+            add_phasors(x, 0, (-cos_h * hz, sin_h * hz, cos_h * hy, -sin_h * hy))
         return carry
 
     acc[...] = jnp.zeros_like(acc)
@@ -454,10 +513,12 @@
             pltpu.VMEM((owners, 8, reach), f32),
         ]
         + [pltpu.VMEM((STEPS,) + face, f32) for face in (x_face, y_face, z_face)] * 2
+        + [pltpu.VMEM((STEPS, 6, max(width_x, width_y), LANES), f32)]
         + [pltpu.VMEM((2, STEPS) + face, f32) for face in (x_face, y_face, z_face)]
+        + [pltpu.VMEM((STEPS, 6, max(width_x, width_y), LANES), f32)]
         + [
-            pltpu.SemaphoreType.DMA((2, 3)),
-            pltpu.SemaphoreType.DMA((STEPS, 2, 3)),
+            pltpu.SemaphoreType.DMA((12,)),
+            pltpu.SemaphoreType.DMA((STEPS, 12)),
             pltpu.SemaphoreType.DMA((3,)),
             pltpu.SemaphoreType.DMA((3,)),
             pltpu.SemaphoreType.DMA((owners,)),

time: 47.5 us -> 39.5 us (0.83)
  Pallas kernels: 44 us -> 36 us
    pallas_call x1, Pallas kernels: 44 us -> 36 us  [shards(): pl.pallas_call(functools.partial(kernel, sizes, slots, reach), out_shape=...]
where the time goes in v3:
time: 39.5 us; the launch traced here: 39.4 us
  Pallas kernels  36 us (91%)
  local copies, waits for them, and re-layouts  2.7 us (7%)
  between operations  0.65 us (2%)
    pallas_call x1, Pallas kernels, shards(): pl.pallas_call(functools.partial(kernel, sizes, slots, reach), out_shape=...  36 us
    unnamed x4, local copies, waits for them, and re-layouts  2.7 us

profile of v3, /device:TPU:0, one launch (start us, length us, event | category | flops | bytes accessed | tf_op | source)
XLA Modules:
  0.0 39.4 jit_solution(13284978213758683537)
XLA Ops:
  0.6 36.0 %shard_map.113 = (f32[6,16,16,128]{3,2,1,0:T(8,128)}, f32[8,256]{1,0:T(8,128)}) custom-call(f32[6,16,16,128]{3,2,1,0:T(8,128)} %fields_ref.1, f32[6,16,16,128]{3,2,1,0:T(8,128)} %pol_ref.1, s32[16,16,128]{2,1,0:T(8,128)} %mat_ref.1, f32[4]{0:T(128)} %omega_ref.1, f32[4]{0:T(128)} %damp_ref.1, f32[4]{0:T(128)} %strength_ref.1, s32[1,4]{1,0:T(1,128)} %count_ref.1, ...), custom_call_target="tpu_custom_call" | custom-call | tf_op jit(solution)/shard_map/pallas_call | solution.py:492
  36.6 0.0 copy-start
  36.7 2.1 %copy.14 = f32[6,16,16,128]{3,2,1,0:T(8,128)} copy(f32[6,16,16,128]{3,2,1,0:T(8,128)} %get-tuple-element.8) | data formatting | bytes 1572864
  38.8 0.0 copy-done
  38.8 0.6 %copy.15 = f32[256,8]{0,1:T(8,128)} copy(f32[256,8]{0,1:T(8,128)S(1)} %bitcast.3) | data formatting | bytes 16384
Async XLA Ops:
  36.6 2.1 %copy-start = (f32[8,256]{1,0:T(8,128)S(1)}, f32[8,256]{1,0:T(8,128)}, u32[]{:S(2)}) copy-start(f32[8,256]{1,0:T(8,128)} %get-tuple-element.5) | copy-start | bytes 24580

commit v4 on v3

--- a/solution.py
+++ b/solution.py
@@ -53,7 +53,7 @@
     out_ref, far_ref,
     ele, mag, pq, coef, acc, folded, coords, spread, parts, dirs, table, blocks, landed,
     e_x, e_y, e_z, h_x, h_y, h_z, edge, sx, sy, sz, edge_out,
-    face_send, face_recv, pair_send, pair_recv, far_send, far_recv,
+    face_send, face_recv, pair_send, pair_recv, far_send, far_recv, in_sem, out_sem,
 ):
     n_x, n_y, n_z = sizes
     half_y = n_y // 2
@@ -72,6 +72,16 @@
             "gz": lax.rem(m, n_z),
         }
 
+    loads = []
+    for c in range(3):
+        loads.append((fields_ref.at[c], ele.at[c, pl.ds(0, width_x)]))
+        loads.append((fields_ref.at[3 + c], mag.at[c, pl.ds(1, width_x)]))
+        loads.append((pol_ref.at[c], pq.at[0, c]))
+        loads.append((pol_ref.at[3 + c], pq.at[1, c]))
+    loads = [pltpu.make_async_copy(a, b, in_sem.at[k]) for k, (a, b) in enumerate(loads)]
+    for copy in loads:
+        copy.start()
+
     for ghost in (e_x, e_y, e_z, h_x, h_y, h_z, edge, edge_out):
         ghost[...] = jnp.zeros_like(ghost)
 
@@ -104,11 +114,6 @@
             )
         )
 
-    for c in range(3):
-        ele[c, pl.ds(0, width_x)] = fields_ref[c]
-        mag[c, pl.ds(1, width_x)] = fields_ref[3 + c]
-        pq[0, c] = pol_ref[c]
-        pq[1, c] = pol_ref[3 + c]
     material = mat_ref[...]
     coefs = [jnp.zeros(material.shape, jnp.float32) for _ in range(3)]
     for m in range(omega_ref.shape[0]):
@@ -188,11 +193,18 @@
 
     phases = STEPS
     share = -(-owners // phases)
+    group = math.gcd(owners // phases, 4) if owners % phases == 0 else 1
 
     def build_share(phase):
-        lax.fori_loop(
-            jnp.minimum(phase * share, owners), jnp.minimum((phase + 1) * share, owners), build, 0
-        )
+        first = jnp.minimum(phase * share, owners)
+        count = jnp.minimum(share, owners - first) // group
+
+        def build_group(i, carry):
+            for r in range(group):
+                build(first + i * group + r, carry)
+            return carry
+
+        lax.fori_loop(0, count, build_group, 0)
 
     lane2 = lax.broadcasted_iota(jnp.int32, (width_y, LANES), 1)
     row2 = lax.broadcasted_iota(jnp.int32, (width_y, LANES), 0)
@@ -375,7 +387,16 @@
         return carry
 
     acc[...] = jnp.zeros_like(acc)
+    for copy in loads:
+        copy.wait()
     lax.fori_loop(0, STEPS, step_body, 0)
+    stores = []
+    for c in range(3):
+        stores.append((ele.at[c, pl.ds(0, width_x)], out_ref.at[c]))
+        stores.append((mag.at[c, pl.ds(1, width_x)], out_ref.at[3 + c]))
+    stores = [pltpu.make_async_copy(a, b, out_sem.at[k]) for k, (a, b) in enumerate(stores)]
+    for copy in stores:
+        copy.start()
     add_electric(math.cos(angle_e[-1]), math.sin(angle_e[-1]))
 
     row_z = lax.broadcasted_iota(jnp.int32, (depth_z, depth_z), 0)
@@ -413,9 +434,6 @@
     ]
     for copy in to_pair:
         copy.start()
-    for c in range(3):
-        out_ref[c] = ele[c, pl.ds(0, width_x)]
-        out_ref[3 + c] = mag[c, pl.ds(1, width_x)]
 
     scale = 1.0 / math.sqrt(n_x * n_y * n_z * TILE_MEAN * TY * depth_z)
     even = lax.rem(lax.broadcasted_iota(jnp.int32, (8, reach), 0), 2) == 0
@@ -452,15 +470,20 @@
         u, v = sums
         blocks[o] = jnp.where(even, u - pltpu.roll(v, 7, 0), u + pltpu.roll(v, 1, 0)) * scale
 
-    def far_step(o, carry):
-        keep_block(o, add_tiles(empty, lax.rem(me + o, owners), 0, 2))
-        far_copy(o).start()
+    bunch = next(size for size in (3, 1) if (owners - 1) % size == 0)
+
+    def far_step(i, carry):
+        turn = [1 + i * bunch + r for r in range(bunch)]
+        all_sums = [add_tiles(empty, lax.rem(me + o, owners), 0, 2) for o in turn]
+        for o, sums in zip(turn, all_sums):
+            keep_block(o, sums)
+            far_copy(o).start()
         return carry
 
     sums = add_tiles(empty, me, 0, 1)
     for copy in to_pair:
         copy.wait()
-    lax.fori_loop(1, owners, far_step, 0)
+    lax.fori_loop(0, (owners - 1) // bunch, far_step, 0)
     keep_block(0, add_tiles(sums, me, 1, 1))
 
     def gather_step(o, total):
@@ -469,6 +492,18 @@
 
     total = lax.fori_loop(1, owners, gather_step, blocks[0])
     far_ref[...] = total
+    for copy in stores:
+        copy.wait()
+
+
+def hand_out(fields_ref, far_ref, fields_out, far_out, sems):
+    pairs = [(fields_ref.at[c], fields_out.at[c]) for c in range(fields_ref.shape[0])]
+    pairs.append((far_ref, far_out))
+    copies = [pltpu.make_async_copy(a, b, sems.at[k]) for k, (a, b) in enumerate(pairs)]
+    for copy in copies:
+        copy.start()
+    for copy in copies:
+        copy.wait()
 
 
 def shards(
@@ -487,6 +522,7 @@
     even_slots = slots + slots % 2
     coord_rows = -(-slots // 8) * 8
     f32 = jnp.float32
+    anywhere = pl.BlockSpec(memory_space=pl.ANY)
     vmem, smem = pl.BlockSpec(memory_space=pltpu.VMEM), pl.BlockSpec(memory_space=pltpu.SMEM)
     x_face, y_face, z_face = (2, width_y, depth_z), (2, width_x, depth_z), (width_y, LANES)
     fields_out, far = pl.pallas_call(
@@ -495,8 +531,8 @@
             jax.ShapeDtypeStruct(fields.shape, f32),
             jax.ShapeDtypeStruct((8, reach), f32),
         ),
-        in_specs=[vmem] * 3 + [smem] * 5 + [vmem] * 2,
-        out_specs=(vmem, vmem),
+        in_specs=[anywhere] * 2 + [vmem] + [smem] * 5 + [vmem] * 2,
+        out_specs=(anywhere, vmem),
         scratch_shapes=[
             pltpu.VMEM((3, width_x + 1, width_y, depth_z), f32),
             pltpu.VMEM((3, width_x + 1, width_y, depth_z), f32),
@@ -523,6 +559,8 @@
             pltpu.SemaphoreType.DMA((3,)),
             pltpu.SemaphoreType.DMA((owners,)),
             pltpu.SemaphoreType.DMA((owners,)),
+            pltpu.SemaphoreType.DMA((12,)),
+            pltpu.SemaphoreType.DMA((6,)),
         ],
         compiler_params=pltpu.CompilerParams(
             collective_id=0, has_side_effects=True, vmem_limit_bytes=56 * 1024 * 1024
@@ -531,6 +569,16 @@
         fields, polarization, material, omega0, damping, strength,
         tile_count, tile_place, dir_angles, order,
     )
+    fields_out, far = pl.pallas_call(
+        hand_out,
+        out_shape=(
+            jax.ShapeDtypeStruct(fields.shape, f32),
+            jax.ShapeDtypeStruct((8, reach), f32),
+        ),
+        in_specs=[anywhere] * 2,
+        out_specs=(anywhere, anywhere),
+        scratch_shapes=[pltpu.SemaphoreType.DMA((fields.shape[0] + 1,))],
+    )(fields_out, far)
     return fields_out, far.T
 
 

time: 39.5 us -> 60 us (1.52)
  Pallas kernels: 36 us -> 59.2 us
  local copies, waits for them, and re-layouts: 2.7 us -> 0 us
    pallas_call x0 -> x1, Pallas kernels: none -> 25.2 us  [shards(): pl.pallas_call(hand_out, out_shape=(jax.ShapeDtypeStruct(fields.shape, f3...]
    unnamed x4 -> x0, local copies, waits for them, and re-layouts: 2.7 us -> none
    pallas_call x1, Pallas kernels: 36 us -> 34 us  [shards(): pl.pallas_call(functools.partial(kernel, sizes, slots, reach), out_shape=...]
where the time goes in v4:
time: 60 us; the launch traced here: 59.9 us
  Pallas kernels  59.2 us (99%)
  between operations  0.64 us (1%)
    pallas_call x1, Pallas kernels, shards(): pl.pallas_call(functools.partial(kernel, sizes, slots, reach), out_shape=...  34 us
    pallas_call x1, Pallas kernels, shards(): pl.pallas_call(hand_out, out_shape=(jax.ShapeDtypeStruct(fields.shape, f3...  25.2 us

profile of v4, /device:TPU:0, one launch (start us, length us, event | category | flops | bytes accessed | tf_op | source)
XLA Modules:
  0.0 59.9 jit_solution(17143194261876529555)
XLA Ops:
  0.6 34.0 %shard_map.113 = (f32[6,16,16,128]{3,2,1,0:T(8,128)}, f32[8,256]{1,0:T(8,128)}) custom-call(f32[6,16,16,128]{3,2,1,0:T(8,128)} %fields_ref.1, f32[6,16,16,128]{3,2,1,0:T(8,128)} %pol_ref.1, s32[16,16,128]{2,1,0:T(8,128)} %mat_ref.1, f32[4]{0:T(128)} %omega_ref.1, f32[4]{0:T(128)} %damp_ref.1, f32[4]{0:T(128)} %strength_ref.1, s32[1,4]{1,0:T(1,128)} %count_ref.1, ...), custom_call_target="tpu_custom_call" | custom-call | tf_op jit(solution)/shard_map/pallas_call | solution.py:528
  34.6 25.2 %shard_map.114 = (f32[6,16,16,128]{3,2,1,0:T(8,128)}, f32[8,256]{1,0:T(8,128)}) custom-call(f32[6,16,16,128]{3,2,1,0:T(8,128)} %get-tuple-element.6.fields_ref, f32[8,256]{1,0:T(8,128)} %get-tuple-element.7.far_ref), custom_call_target="tpu_custom_call" | custom-call | tf_op jit(solution)/shard_map/pallas_call | solution.py:572

commit v5 on v4

--- a/solution.py
+++ b/solution.py
@@ -493,16 +493,6 @@
     total = lax.fori_loop(1, owners, gather_step, blocks[0])
     far_ref[...] = total
     for copy in stores:
-        copy.wait()
-
-
-def hand_out(fields_ref, far_ref, fields_out, far_out, sems):
-    pairs = [(fields_ref.at[c], fields_out.at[c]) for c in range(fields_ref.shape[0])]
-    pairs.append((far_ref, far_out))
-    copies = [pltpu.make_async_copy(a, b, sems.at[k]) for k, (a, b) in enumerate(pairs)]
-    for copy in copies:
-        copy.start()
-    for copy in copies:
         copy.wait()
 
 
@@ -569,16 +559,6 @@
         fields, polarization, material, omega0, damping, strength,
         tile_count, tile_place, dir_angles, order,
     )
-    fields_out, far = pl.pallas_call(
-        hand_out,
-        out_shape=(
-            jax.ShapeDtypeStruct(fields.shape, f32),
-            jax.ShapeDtypeStruct((8, reach), f32),
-        ),
-        in_specs=[anywhere] * 2,
-        out_specs=(anywhere, anywhere),
-        scratch_shapes=[pltpu.SemaphoreType.DMA((fields.shape[0] + 1,))],
-    )(fields_out, far)
     return fields_out, far.T
 
 

time: 60 us -> 37.5 us (0.62)
  Pallas kernels: 59.2 us -> 34 us
  local copies, waits for them, and re-layouts: 0 us -> 2.7 us
    pallas_call x1 -> x0, Pallas kernels: 25.2 us -> none  [shards(): pl.pallas_call(hand_out, out_shape=(jax.ShapeDtypeStruct(fields.shape, f3...]
    unnamed x0 -> x4, local copies, waits for them, and re-layouts: none -> 2.7 us
where the time goes in v5:
time: 37.5 us; the launch traced here: 37.3 us
  Pallas kernels  34 us (91%)
  local copies, waits for them, and re-layouts  2.7 us (7%)
  between operations  0.65 us (2%)
    pallas_call x1, Pallas kernels, shards(): pl.pallas_call(functools.partial(kernel, sizes, slots, reach), out_shape=...  34 us
    unnamed x4, local copies, waits for them, and re-layouts  2.7 us

profile of v5, /device:TPU:0, one launch (start us, length us, event | category | flops | bytes accessed | tf_op | source)
XLA Modules:
  0.0 37.3 jit_solution(15632574020052052323)
XLA Ops:
  0.6 34.0 %shard_map.113 = (f32[6,16,16,128]{3,2,1,0:T(8,128)}, f32[8,256]{1,0:T(8,128)}) custom-call(f32[6,16,16,128]{3,2,1,0:T(8,128)} %fields_ref.1, f32[6,16,16,128]{3,2,1,0:T(8,128)} %pol_ref.1, s32[16,16,128]{2,1,0:T(8,128)} %mat_ref.1, f32[4]{0:T(128)} %omega_ref.1, f32[4]{0:T(128)} %damp_ref.1, f32[4]{0:T(128)} %strength_ref.1, s32[1,4]{1,0:T(1,128)} %count_ref.1, ...), custom_call_target="tpu_custom_call" | custom-call | tf_op jit(solution)/shard_map/pallas_call | solution.py:518
  34.6 0.0 copy-start
  34.6 2.1 %copy.14 = f32[6,16,16,128]{3,2,1,0:T(8,128)} copy(f32[6,16,16,128]{3,2,1,0:T(8,128)} %get-tuple-element.8) | data formatting | bytes 1572864
  36.7 0.0 copy-done
  36.8 0.6 %copy.15 = f32[256,8]{0,1:T(8,128)} copy(f32[256,8]{0,1:T(8,128)S(1)} %bitcast.3) | data formatting | bytes 16384
Async XLA Ops:
  34.6 2.1 %copy-start = (f32[8,256]{1,0:T(8,128)S(1)}, f32[8,256]{1,0:T(8,128)}, u32[]{:S(2)}) copy-start(f32[8,256]{1,0:T(8,128)} %get-tuple-element.5) | copy-start | bytes 24580
